TPU v7x, 768 devices: a whole 4x8x12 slice. The times are simulated.
768 devices in a mesh: slab: 12 (over z), sub: 64 (over x, y, core).
Axes of the slice: x: 4, y: 8, z: 12, core: 2. Of those that a mesh axis runs over, the one named last changes fastest.
Arguments:
- fields: float32 [5, 512, 768, 128], P(None, None, ('slab', 'sub')), may hold values from -6 to 6
- metric: float32 [3, 768, 128], P(None, ('slab', 'sub')), may hold values from 0.5 to 2
- diffusivity: float32 [5], replicated, may hold values from 0.0001 to 0.001
- joule_heat: float32 [512, 768, 128], P(None, ('slab', 'sub')), may hold values from 0.5 to 5
- face_flip: int32 [768], P(('slab', 'sub')), may hold values from 0 to 1
- coarse_decay: float32 [8, 768, 128], P(None, ('slab', 'sub')), may hold values from 0 to 1
Outputs:
- advanced: float32 [5, 512, 768, 128], P(None, None, ('slab', 'sub'))
- pressure: float32 [512, 768, 128], P(None, ('slab', 'sub'))
All inputs are finite; a program needn't handle non-finite values.
Results may differ from a plain program's by a relative error of at most 0.0002.
Values sent between devices are 32-bit elements; how exact they have to be, the bound alone decides.
A program may use at most 32 MiB of HBM per device.

v0:
```python
import jax
import jax.numpy as jnp
import numpy as np
from jax import lax
from jax.sharding import PartitionSpec as P

HIGHEST = lax.Precision.HIGHEST
FORMS = ("ia,fajkcl->fijkcl", "ja,fiakcl->fijkcl", "ka,fijacl->fijkcl")


def padded_2(shard, sides, width):
    for axis, dim in sides:
        devices, length = (lax.axis_size(axis), shard.shape[dim])
        up = [(i, (i + 1) % devices) for i in range(devices - 1)]
        down = [(j, i) for i, j in up]
        last = lax.slice_in_dim(shard, length - width, length, axis=dim)
        first = lax.slice_in_dim(shard, 0, width, axis=dim)
        before = lax.ppermute(last, axis, up)
        after = lax.ppermute(first, axis, down)
        shard = jnp.concatenate([before, shard, after], axis=dim)
    return shard


def carried_in(value, axis, join, neutral, backward):
    count, mine = (lax.axis_size(axis), lax.axis_index(axis))
    pieces = jax.tree.map(lambda part: lax.all_gather(part, axis), value)
    if backward:
        pieces = jax.tree.map(lambda part: part[::-1], pieces)
        mine = count - 1 - mine
    subtotal = jax.tree.map(
        lambda part, zero: jnp.full_like(part, 0) + jnp.asarray(zero, part.dtype), value, neutral
    )

    def hop(position, subtotal):
        longer = join(subtotal, jax.tree.map(lambda part: part[position], pieces))
        return jax.tree.map(lambda new, old: jnp.where(position < mine, new, old), longer, subtotal)

    return lax.fori_loop(0, count - 1, hop, subtotal)


def spread_2(value, axis, source):
    kept = jnp.where(lax.axis_index(axis) == source, value, 0).astype(value.dtype)
    return lax.psum(kept, axis)


def spectral_tables():
    points = np.cos(np.pi * np.arange(8) / 7.0)
    endings = np.ones(8)
    endings[0] = 2.0
    endings[7] = 2.0
    weighted = endings * (-1.0) ** np.arange(8)
    quotient = weighted[:, None] / weighted[None, :]
    spacing = points[:, None] - points[None, :] + np.eye(8)
    derive = quotient / spacing
    derive = derive - np.eye(8) * np.sum(derive, axis=1)[:, None]
    column_sq = np.sum(derive * derive, axis=0)
    index_all = np.arange(512)
    digits = (index_all // 64, index_all // 8 % 8, index_all % 8)
    diagonal = np.stack([column_sq[digit_set] for digit_set in digits])
    halves = np.stack([(1.0 - points) / 2.0, (1.0 + points) / 2.0])
    vertex = np.ones((8, 512))
    for corner in range(8):
        for position in range(3):
            vertex[corner] = vertex[corner] * halves[corner >> 2 - position & 1][digits[position]]
    return (
        jnp.asarray(derive, jnp.float32),
        jnp.asarray(diagonal, jnp.float32),
        jnp.asarray(vertex, jnp.float32),
    )


def along(field, derive, direction):
    leading = field.shape[0]
    cube_view = field.reshape((leading, 8, 8, 8) + field.shape[2:])
    result = jnp.einsum(FORMS[direction], derive, cube_view, precision=HIGHEST)
    return result.reshape(field.shape)


def advance(fields, metric, diffusivity, joule_heat, derive):
    scales = [metric[direction][None, None] for direction in range(3)]
    slopes = [scales[direction] * along(fields, derive, direction) for direction in range(3)]
    carried = fields[0:1] * slopes[0] + fields[1:2] * slopes[1] + fields[2:3] * slopes[2]
    spread = -(
        scales[0] * along(slopes[0], derive.T, 0)
        + scales[1] * along(slopes[1], derive.T, 1)
        + scales[2] * along(slopes[2], derive.T, 2)
    )
    heat_in = joule_heat * (1.0 + 0.5 * jnp.tanh(fields[3])) * jax.nn.sigmoid(-fields[4])
    lifting = 0.3 * fields[3] - 0.5 * jax.nn.sigmoid(fields[4])
    nothing = jnp.zeros_like(heat_in)
    source = jnp.stack([nothing, lifting, nothing, heat_in, 0.2 * heat_in])
    stepped = fields - 0.01 * carried + diffusivity[:, None, None, None] * spread + 0.05 * source
    node_k = jnp.arange(512) % 8
    inside = ((node_k > 0) & (node_k < 7)).astype(jnp.float32)
    keeper = jnp.stack([inside, inside, inside, jnp.ones_like(inside), jnp.ones_like(inside)])
    return stepped * keeper[:, :, None, None]


def divergence(velocity, metric, derive):
    summed = metric[0][None, None] * along(velocity[0:1], derive, 0)
    summed = summed + metric[1][None, None] * along(velocity[1:2], derive, 1)
    summed = summed + metric[2][None, None] * along(velocity[2:3], derive, 2)
    return summed


def pressure_pair(source, metric, derive, diagonal):
    denominator = 1.0
    for direction in range(3):
        denominator = (
            denominator
            + metric[direction][None, None] ** 2 * diagonal[direction][None, :, None, None]
        )
    weight = 0.5 / denominator
    first_guess = weight * source
    applied = first_guess
    for direction in range(3):
        scale_now = metric[direction][None, None]
        applied = applied + scale_now * along(
            scale_now * along(first_guess, derive, direction), derive.T, direction
        )
    return jnp.concatenate([first_guess, source - applied], axis=0)


def join_lateral(field):
    cube_view = field.reshape((field.shape[0], 8, 8, 8) + field.shape[2:])
    lower_face = cube_view[:, :, 0]
    upper_face = cube_view[:, :, 7]
    shared = 0.5 * (lower_face + jnp.roll(upper_face, 1, axis=-1))
    joined = jnp.concatenate(
        [shared[:, :, None], cube_view[:, :, 1:7], jnp.roll(shared, -1, axis=-1)[:, :, None]],
        axis=2,
    )
    return joined.reshape(field.shape)


def oriented(face, flipped):
    face_grid = face.reshape((face.shape[0], 8, 8) + face.shape[2:])
    turned = face_grid[:, :, ::-1].reshape(face.shape)
    return jnp.where(flipped, turned, face)


def outgoing(field, flipped):
    return jnp.concatenate([oriented(field[:, :64], flipped), field[:, 448:]], axis=2)


def chain_faces(field, padded, flipped, at_start, at_end):
    first_face = field[:, :64]
    last_face = field[:, 448:]
    new_first = jnp.where(
        at_start, first_face, 0.5 * (first_face + oriented(padded[:, :, 0:1], flipped))
    )
    new_last = jnp.where(at_end, last_face, 0.5 * (last_face + padded[:, :, 3:4]))
    return jnp.concatenate([new_first, field[:, 64:448], new_last], axis=1)


def chain_step(earlier, later):
    return (earlier[0] * later[0], later[0] * earlier[1] + later[1])


def local(fields, metric, diffusivity, joule_heat, face_flip, coarse_decay):
    derive, diagonal, vertex = spectral_tables()
    where_at = lax.axis_index(("slab", "sub"))
    chain_size = lax.axis_size(("slab", "sub"))
    block_size = lax.axis_size("sub")
    at_start = where_at == 0
    at_end = where_at == chain_size - 1
    flipped = face_flip[0] == 1
    stepped = join_lateral(advance(fields, metric, diffusivity, joule_heat, derive))
    moving = padded_2(outgoing(stepped[0:3], flipped), ((("slab", "sub"), 2),), 1)
    scalar = padded_2(outgoing(stepped[3:5], flipped), ((("slab", "sub"), 2),), 1)
    padded = jnp.concatenate([moving, scalar], axis=0)
    advanced = chain_faces(stepped, padded, flipped, at_start, at_end)
    source = divergence(advanced[0:3], metric, derive)
    press_pair = join_lateral(pressure_pair(source, metric, derive, diagonal))
    press_padded = padded_2(outgoing(press_pair, flipped), ((("slab", "sub"), 2),), 1)
    press_pair = chain_faces(press_pair, press_padded, flipped, at_start, at_end)
    coarse_rhs = jnp.einsum("mn,ncl->mcl", vertex / 64.0, press_pair[1], precision=HIGHEST)
    gain_root = jnp.sqrt((1.0 - coarse_decay) * (1.0 + coarse_decay))
    identity = (jnp.ones_like(coarse_decay), jnp.zeros_like(coarse_decay))
    own_forward = (coarse_decay, gain_root * coarse_rhs)
    inner_fwd = carried_in(own_forward, "sub", chain_step, identity, False)
    whole_fwd = chain_step(inner_fwd, own_forward)
    total_fwd = (
        spread_2(whole_fwd[0], "sub", block_size - 1),
        spread_2(whole_fwd[1], "sub", block_size - 1),
    )
    outer_fwd = carried_in(total_fwd, "slab", chain_step, identity, False)
    prefix = chain_step(outer_fwd, inner_fwd)
    forward = coarse_decay * prefix[1] + own_forward[1]
    own_backward = (coarse_decay, gain_root * forward)
    inner_back = carried_in(own_backward, "sub", chain_step, identity, True)
    whole_back = chain_step(inner_back, own_backward)
    total_back = (spread_2(whole_back[0], "sub", 0), spread_2(whole_back[1], "sub", 0))
    outer_back = carried_in(total_back, "slab", chain_step, identity, True)
    suffix = chain_step(outer_back, inner_back)
    backward = coarse_decay * suffix[1] + own_backward[1]
    pressure = press_pair[0] + jnp.einsum("mn,mcl->ncl", vertex, backward, precision=HIGHEST)
    return (advanced, pressure)


def solution(mesh):
    in_specs = (
        P(None, None, ("slab", "sub"), None),
        P(None, ("slab", "sub"), None),
        P(),
        P(None, ("slab", "sub"), None),
        P(("slab", "sub")),
        P(None, ("slab", "sub"), None),
    )
    out_specs = (P(None, None, ("slab", "sub"), None), P(None, ("slab", "sub"), None))
    return jax.shard_map(local, mesh=mesh, in_specs=in_specs, out_specs=out_specs, check_vma=False)
```

profile of v0, /device:TPU:64, one launch (start us, length us, event | category | flops | bytes accessed | tf_op | source)
XLA Modules:
  0.0 529.7 jit_solution(11280588866032584717)
XLA Ops:
  0.7 3.3 convolution_bitcast_fusion.3
  3.9 1.3 convolution_bitcast_fusion.2
  5.2 1.2 fusion.83
  7.4 1.3 convolution_bitcast_fusion.1
  9.1 1.3 convolution_bitcast_fusion
  11.6 1.3 fusion
  13.1 1.6 fusion.8
  16.3 1.9 collective-permute-start.2
  18.2 7.9 %collective-permute-start.3 = (f32[2,64,1,128]{3,1,2,0:T(8,128)S(1)}, f32[2,64,1,128]{3,1,2,0:T(8,128)S(1)}, u32[]{:S(2)}, u32[]{:S(2)}) collective-permute-start(f32[2,64,1,128]{3,1,2,0:T(8,128)S(1)} %get-tuple-element.627), channel_id=1, source_target_pairs={{1,0},{2,1},{3,2},{4,3},{5,4},{6,5},{7,6},{8,7},{9,8},{10,9},{11,1... | collective-permute-start | bytes 196616 | tf_op jit(solution)/shard_map/ppermute | solution.py:19
  26.3 1.9 collective-permute-start
  28.2 8.0 %collective-permute-start.1 = (f32[3,64,1,128]{3,1,0,2:T(8,128)S(1)}, f32[3,64,1,128]{3,1,0,2:T(8,128)S(1)}, u32[]{:S(2)}, u32[]{:S(2)}) collective-permute-start(f32[3,64,1,128]{3,1,0,2:T(8,128)S(1)} %get-tuple-element.621), channel_id=1, source_target_pairs={{1,0},{2,1},{3,2},{4,3},{5,4},{6,5},{7,6},{8,7},{9,8},{10,9},{11,1... | collective-permute-start | bytes 294920 | tf_op jit(solution)/shard_map/ppermute | solution.py:19
  36.4 1.8 collective-permute-done.1
  38.6 0.6 copy-done.3
  39.9 0.7 fusion.24
  41.9 0.6 fusion.26
  43.7 0.7 fusion.32
  45.5 1.9 collective-permute-start.4
  47.5 7.9 %collective-permute-start.5 = (f32[2,64,1,128]{3,1,2,0:T(8,128)S(1)}, f32[2,64,1,128]{3,1,2,0:T(8,128)S(1)}, u32[]{:S(2)}, u32[]{:S(2)}) collective-permute-start(f32[2,64,1,128]{3,1,2,0:T(8,128)S(1)} %bitcast_select_fusion.2), channel_id=1, source_target_pairs={{1,0},{2,1},{3,2},{4,3},{5,4},{6,5},{7,6},{8,7},{9,8},{10,9},{11,1... | collective-permute-start | bytes 196616 | tf_op jit(solution)/shard_map/ppermute | solution.py:19
  55.5 36.9 %all-gather = f32[512,1,128]{2,1,0:T(1,128)S(1)} all-gather(f32[8,1,128]{2,1,0:T(1,128)S(1)} %copy-done.5), channel_id=2, replica_groups=mesh['slab'=12,'sub'=64] {'sub'}, dimensions={0}, use_global_device_ids=true | all-gather | bytes 266240 | tf_op jit(solution)/shard_map/all_gather | solution.py:26
  93.3 37.1 %all-gather.1 = f32[512,1,128]{2,0,1:T(8,128)S(1)} all-gather(f32[8,1,128]{2,0,1:T(8,128)S(1)} %fusion.33), channel_id=3, replica_groups=mesh['slab'=12,'sub'=64] {'sub'}, dimensions={0}, use_global_device_ids=true | all-gather | bytes 266240 | tf_op jit(solution)/shard_map/all_gather | solution.py:26
  130.5 4.0 while.60
  134.5 128.9 %all-reduce.1 = (f32[1,8,1,128]{3,1,2,0:T(8,128)S(1)}, f32[1,8,1,128]{3,1,2,0:T(8,128)S(1)}) all-reduce(f32[1,8,1,128]{3,1,2,0:T(8,128)S(1)} %get-tuple-element.639, f32[1,8,1,128]{3,1,2,0:T(8,128)S(1)} %get-tuple-element.638), channel_id=1, replica_groups=mesh['slab'=12,'sub'=64] {'sub'}, use_global_device_ids=true, to_apply=%region_2.3 | all-reduce | flops 2048 | bytes 16384 | tf_op jit(solution)/shard_map/psum | solution.py:43
  263.4 31.0 %all_gather.49 = f32[12,8,1,128]{3,1,2,0:T(8,128)S(1)} all-gather(f32[1,8,1,128]{3,1,2,0:T(8,128)S(1)} %get-tuple-element.596), channel_id=1, replica_groups=mesh['slab'=12,'sub'=64] {'slab'}, dimensions={0}, use_global_device_ids=true | all-gather | bytes 53248 | tf_op jit(solution)/shard_map/all_gather | solution.py:26
  294.4 21.0 %all_gather.51 = f32[12,8,1,128]{3,1,2,0:T(8,128)S(1)} all-gather(f32[1,8,1,128]{3,1,2,0:T(8,128)S(1)} %get-tuple-element.597), channel_id=1, replica_groups=mesh['slab'=12,'sub'=64] {'slab'}, dimensions={0}, use_global_device_ids=true | all-gather | bytes 53248 | tf_op jit(solution)/shard_map/all_gather | solution.py:26
  315.4 0.6 while.61
  316.1 36.9 %all-gather.2 = f32[512,1,128]{2,0,1:T(8,128)S(1)} all-gather(f32[8,1,128]{2,0,1:T(8,128)S(1)} %add_multiply_fusion), channel_id=4, replica_groups=mesh['slab'=12,'sub'=64] {'sub'}, dimensions={0}, use_global_device_ids=true | all-gather | bytes 266240 | tf_op jit(solution)/shard_map/all_gather | solution.py:26
  353.0 4.0 while.62
  357.0 128.9 %all-reduce = (f32[1,8,1,128]{3,1,2,0:T(8,128)S(1)}, f32[1,8,1,128]{3,1,2,0:T(8,128)S(1)}) all-reduce(f32[1,8,1,128]{3,1,2,0:T(8,128)S(1)} %get-tuple-element.637, f32[1,8,1,128]{3,1,2,0:T(8,128)S(1)} %get-tuple-element.636), channel_id=1, replica_groups=mesh['slab'=12,'sub'=64] {'sub'}, use_global_device_ids=true, to_apply=%region_8.9 | all-reduce | flops 2048 | bytes 16384 | tf_op jit(solution)/shard_map/psum | solution.py:43
  485.9 21.9 %all_gather.55 = f32[12,8,1,128]{3,1,2,0:T(8,128)S(1)} all-gather(f32[1,8,1,128]{3,1,2,0:T(8,128)S(1)} %get-tuple-element.594), channel_id=1, replica_groups=mesh['slab'=12,'sub'=64] {'slab'}, dimensions={0}, use_global_device_ids=true | all-gather | bytes 53248 | tf_op jit(solution)/shard_map/all_gather | solution.py:26
  507.9 19.9 %all_gather.57 = f32[12,8,1,128]{3,1,2,0:T(8,128)S(1)} all-gather(f32[1,8,1,128]{3,1,2,0:T(8,128)S(1)} %get-tuple-element.595), channel_id=1, replica_groups=mesh['slab'=12,'sub'=64] {'slab'}, dimensions={0}, use_global_device_ids=true | all-gather | bytes 53248 | tf_op jit(solution)/shard_map/all_gather | solution.py:26
  527.8 0.6 while.63
  528.4 1.3 convolution_add_fusion
  (407 shorter events, 13.6 us)
Async XLA Ops:
  0.6 3.3 copy-start
  0.6 3.3 copy-start.4
  6.4 0.7 copy-start.11
  10.4 1.0 copy-start.2
  11.6 1.5 copy-start.12
  16.3 20.0 %collective-permute-start.2 = (f32[2,64,1,128]{3,1,2,0:T(8,128)S(1)}, f32[2,64,1,128]{3,1,2,0:T(8,128)S(1)}, u32[]{:S(2)}, u32[]{:S(2)}) collective-permute-start(f32[2,64,1,128]{3,1,2,0:T(8,128)S(1)} %get-tuple-element.626), channel_id=1, source_target_pairs={{0,1},{1,2},{2,3},{3,4},{4,5},{5,6},{6,7},{7,8},{8,9},{9,10},{10,1... | collective-permute-start | bytes 196616 | tf_op jit(solution)/shard_map/ppermute | solution.py:18
  18.2 18.1 %collective-permute-start.3 = (f32[2,64,1,128]{3,1,2,0:T(8,128)S(1)}, f32[2,64,1,128]{3,1,2,0:T(8,128)S(1)}, u32[]{:S(2)}, u32[]{:S(2)}) collective-permute-start(f32[2,64,1,128]{3,1,2,0:T(8,128)S(1)} %get-tuple-element.627), channel_id=1, source_target_pairs={{1,0},{2,1},{3,2},{4,3},{5,4},{6,5},{7,6},{8,7},{9,8},{10,9},{11,1... | collective-permute-start | bytes 196616 | tf_op jit(solution)/shard_map/ppermute | solution.py:19
  26.3 10.2 %collective-permute-start = (f32[3,64,1,128]{3,1,0,2:T(8,128)S(1)}, f32[3,64,1,128]{3,1,0,2:T(8,128)S(1)}, u32[]{:S(2)}, u32[]{:S(2)}) collective-permute-start(f32[3,64,1,128]{3,1,0,2:T(8,128)S(1)} %get-tuple-element.620), channel_id=1, source_target_pairs={{0,1},{1,2},{2,3},{3,4},{4,5},{5,6},{6,7},{7,8},{8,9},{9,10},{10,1... | collective-permute-start | bytes 294920 | tf_op jit(solution)/shard_map/ppermute | solution.py:18
  28.2 10.1 %collective-permute-start.1 = (f32[3,64,1,128]{3,1,0,2:T(8,128)S(1)}, f32[3,64,1,128]{3,1,0,2:T(8,128)S(1)}, u32[]{:S(2)}, u32[]{:S(2)}) collective-permute-start(f32[3,64,1,128]{3,1,0,2:T(8,128)S(1)} %get-tuple-element.621), channel_id=1, source_target_pairs={{1,0},{2,1},{3,2},{4,3},{5,4},{6,5},{7,6},{8,7},{9,8},{10,9},{11,1... | collective-permute-start | bytes 294920 | tf_op jit(solution)/shard_map/ppermute | solution.py:19
  38.5 1.5 copy-start.1
  38.5 0.7 copy-start.3
  38.5 2.1 copy-start.6
  38.6 2.1 copy-start.7
  38.6 2.1 copy-start.8
  45.3 10.2 %copy-start.5 = (f32[8,1,128]{2,1,0:T(1,128)S(1)}, f32[8,1,128]{2,1,0:T(1,128)}, u32[]{:S(2)}) copy-start(f32[8,1,128]{2,1,0:T(1,128)} %param.22) | copy-start | bytes 12292
  45.5 46.9 %collective-permute-start.4 = (f32[2,64,1,128]{3,1,2,0:T(8,128)S(1)}, f32[2,64,1,128]{3,1,2,0:T(8,128)S(1)}, u32[]{:S(2)}, u32[]{:S(2)}) collective-permute-start(f32[2,64,1,128]{3,1,2,0:T(8,128)S(1)} %get-tuple-element.624), channel_id=1, source_target_pairs={{0,1},{1,2},{2,3},{3,4},{4,5},{5,6},{6,7},{7,8},{8,9},{9,10},{10,1... | collective-permute-start | bytes 196616 | tf_op jit(solution)/shard_map/ppermute | solution.py:18
  47.5 45.0 %collective-permute-start.5 = (f32[2,64,1,128]{3,1,2,0:T(8,128)S(1)}, f32[2,64,1,128]{3,1,2,0:T(8,128)S(1)}, u32[]{:S(2)}, u32[]{:S(2)}) collective-permute-start(f32[2,64,1,128]{3,1,2,0:T(8,128)S(1)} %bitcast_select_fusion.2), channel_id=1, source_target_pairs={{1,0},{2,1},{3,2},{4,3},{5,4},{6,5},{7,6},{8,7},{9,8},{10,9},{11,1... | collective-permute-start | bytes 196616 | tf_op jit(solution)/shard_map/ppermute | solution.py:19
  92.4 0.7 copy-start.10
  134.5 394.0 %copy-start.9 = (f32[8,512]{1,0:T(8,128)S(1)}, f32[8,512]{1,0:T(8,128)}, u32[]{:S(2)}) copy-start(f32[8,512]{1,0:T(8,128)} %constant.161.clone) | copy-start | bytes 49156
where the time goes:
time: 530 us
  blocking collectives  463 us (87%)
  starting transfers between devices  29.6 us (6%)
  matrix products  15.6 us (3%)
  other arithmetic  6.82 us (1%)
  local copies, waits for them, and re-layouts  6.15 us (1%)
    psum x2, blocking collectives, spread_2(): return lax.psum(kept, axis)  258 us
    all_gather x7, blocking collectives, carried_in(): pieces = jax.tree.map(lambda part: lax.all_gather(part, axis), value)  205 us
    ppermute x3, starting transfers between devices, padded_2(): after = lax.ppermute(first, axis, down)  23.9 us
    dot_general x15, matrix products, along(): result = jnp.einsum(FORMS[direction], derive, cube_view, precision=HIGHEST)  14.1 us
  transfers between devices with their start and end apart: 6, of which 1 were waited for; matrix products, arithmetic and copies ran while one was open for 0% of the time, Pallas kernels for 0%

commit v1 on v0

v1 whole, which is shorter than its diff:
```python
import functools

import jax
import jax.numpy as jnp
import numpy as np
from jax import lax
from jax.experimental import pallas as pl
from jax.experimental.pallas import tpu as pltpu
from jax.sharding import PartitionSpec as P

MESH = pl.DeviceIdType.MESH
F32 = jnp.float32

POINTS = np.cos(np.pi * np.arange(8) / 7.0)


def derivative():
    endings = np.ones(8)
    endings[0] = endings[7] = 2.0
    weighted = endings * (-1.0) ** np.arange(8)
    spacing = POINTS[:, None] - POINTS[None, :] + np.eye(8)
    derive = weighted[:, None] / weighted[None, :] / spacing
    return derive - np.eye(8) * np.sum(derive, axis=1)[:, None]


D = derivative()
K = D.T @ D
COLUMN_SQ = np.sum(D * D, axis=0)
H = np.stack([(1.0 - POINTS) / 2.0, (1.0 + POINTS) / 2.0])


def half_tables(matrix):
    even = (matrix[:4, :4] + matrix[:4, :3:-1]) / 2.0
    odd = (matrix[:4, :4] - matrix[:4, :3:-1]) / 2.0
    return even.tolist(), odd.tolist()


D_EVEN, D_ODD = half_tables(D)
K_EVEN, K_ODD = half_tables(K)


def dot4(row, parts):
    total = row[0] * parts[0]
    for a in range(1, 4):
        total = total + row[a] * parts[a]
    return total


def split(x):
    return [x[a] + x[7 - a] for a in range(4)], [x[a] - x[7 - a] for a in range(4)]


def apply_d(even, odd, p):
    from_even, from_odd = dot4(D_EVEN[p], even), dot4(D_ODD[p], odd)
    return from_odd + from_even, from_odd - from_even


def apply_k(even, odd, p):
    from_even, from_odd = dot4(K_EVEN[p], even), dot4(K_ODD[p], odd)
    return from_even + from_odd, from_even - from_odd


def ring(n, d):
    return min(d, n - d)


def kernel(
    sizes, fields, heat, metric, diffusivity, flip, decay, adv_out, prs_out,
    f, q, met, dif, flp, dec, s, u, tt, dv, fg, res, wgt, proj, kept,
    face_l, face_r, got_l, got_r, pface_l, pface_r, pgot_l, pgot_r,
    near_out, near, mine, partner, chips, stat, pre, slabs, zstat,
    load_sem, out_sem, face_send, face_recv, pface_send, pface_recv, near_send, near_recv,
    pair_sem, chip_sem, stat_sem, slab_sem, zstat_sem,
):
    nz, nx, ny = sizes
    chips_n = nx * ny
    sub_n = 2 * chips_n
    total = nz * sub_n
    z, sub = lax.axis_index("slab"), lax.axis_index("sub")
    core = lax.rem(sub, 2)
    chip = lax.div(sub, 2)
    cx, cy = lax.div(chip, ny), lax.rem(chip, ny)
    here = z * sub_n + sub
    at_start, at_end = here == 0, here == total - 1
    side = 2 * core - 1

    def at(position):
        position = lax.rem(position + total, total)
        return (lax.div(position, sub_n), lax.rem(position, sub_n))

    other_core = (z, sub - side)
    before, after = at(here - 1), at(here + 1)
    outer, outer_two, inner_two = at(here + side), at(here + 2 * side), at(here - 2 * side)
    chip_order = sorted(range(1, chips_n), key=lambda d: -(ring(nx, d // ny) + ring(ny, d % ny)))
    slab_order = sorted(range(1, nz), key=lambda d: -ring(nz, d))

    def chip_peer(d):
        px, py = lax.rem(cx + d // ny, nx), lax.rem(cy + d % ny, ny)
        return (z, (px * ny + py) * 2 + core)

    def slab_peer(d):
        return (lax.rem(z + d, nz), sub)

    def send(src, dst, send_sem, recv_sem, device):
        copy = pltpu.make_async_remote_copy(
            src_ref=src, dst_ref=dst, send_sem=send_sem, recv_sem=recv_sem,
            device_id=device, device_id_type=MESH,
        )
        copy.start()
        return copy

    def wait_bytes(ref, sem):
        pltpu.make_async_copy(ref, ref, sem).wait()

    loads = [
        pltpu.make_async_copy(decay, dec, load_sem.at[0]),
        pltpu.make_async_copy(metric, met, load_sem.at[1]),
        pltpu.make_async_copy(flip, flp, load_sem.at[2]),
        pltpu.make_async_copy(diffusivity, dif, load_sem.at[3]),
        pltpu.make_async_copy(fields, f, load_sem.at[4]),
        pltpu.make_async_copy(heat, q, load_sem.at[5]),
    ]
    for copy in loads:
        copy.start()

    barrier = pltpu.get_barrier_semaphore()
    targets = [other_core, outer, inner_two]
    targets += [chip_peer(d) for d in chip_order] + [slab_peer(d) for d in slab_order]
    for device in targets:
        pl.semaphore_signal(barrier, inc=1, device_id=device, device_id_type=MESH)

    for copy in loads:
        copy.wait()

    row = lax.broadcasted_iota(jnp.int32, (8, 128), 0)
    zero = jnp.zeros((8, 128), F32)
    wall = jnp.where((row == 0) | (row == 7), 0.0, 1.0)
    turned = (zero + flp[0].astype(F32)) == 1.0
    m = [jnp.broadcast_to(met[d], (8, 128)) for d in range(3)]
    msq = [m[d] * m[d] for d in range(3)]

    def by_row(values):
        out = zero + float(values[7])
        for k in range(7):
            out = jnp.where(row == k, float(values[k]), out)
        return out

    def reverse(x):
        half = pltpu.roll(x, 4, 0)
        pairs = jnp.where(lax.rem(row, 4) < 2, pltpu.roll(half, 6, 0), pltpu.roll(half, 2, 0))
        return jnp.where(lax.rem(row, 2) == 0, pltpu.roll(pairs, 7, 0), pltpu.roll(pairs, 1, 0))

    def oriented(x):
        return jnp.where(turned, reverse(x), x)

    def tile(ref, base):
        return ref.at[pl.ds(pl.multiple_of(base, 8), 8), :]

    def strided(ref, base, k):
        return ref[pl.ds(base + k, 8, stride=8), :]

    def start_plane(i):
        def line(j, carry):
            at_row = i * 64 + j * 8
            x = [tile(f, n * 512 + at_row)[...] for n in range(5)]
            warm = jnp.tanh(x[3])
            bubbles = jnp.tanh(0.5 * x[4])
            heating = tile(q, at_row)[...] * (0.05 + 0.025 * warm) * (0.5 - 0.5 * bubbles)
            lifting = 0.015 * x[3] - 0.0125 - 0.0125 * bubbles
            added = [x[0], x[1] + lifting, x[2], x[3] + heating, x[4] + 0.2 * heating]
            for n in range(5):
                tile(s, n * 512 + at_row)[...] = added[n]
            for n in range(3):
                tile(u, n * 512 + at_row)[...] = 0.01 * m[n] * x[n]
            return carry

        lax.fori_loop(0, 8, line, 0, unroll=2)

    def step_plane(n, i):
        at_row = i * 64
        base = n * 512 + at_row
        rate = dif[n]
        c1, c2 = rate * msq[1], rate * msq[2]
        even, odd = split([strided(f, base, k) for k in range(8)])
        for p in range(4):
            slopes, bends = apply_d(even, odd, p), apply_k(even, odd, p)
            for k, slope, bend in zip((p, 7 - p), slopes, bends):
                tt[8 * k : 8 * k + 8, :] = strided(u, 1024 + at_row, k) * slope + c2 * bend
        even, odd = split([tile(f, base + 8 * j)[...] for j in range(8)])
        for p in range(4):
            slopes, bends = apply_d(even, odd, p), apply_k(even, odd, p)
            for j, slope, bend in zip((p, 7 - p), slopes, bends):
                gone = tile(u, 512 + at_row + 8 * j)[...] * slope + c1 * bend
                gone = gone + strided(tt, 0, j)
                tile(s, base + 8 * j)[...] = tile(s, base + 8 * j)[...] - gone

    def step_lines(n, pairs):
        c0 = dif[n] * msq[0]
        keep = jnp.where(zero + (n < 3).astype(F32) > 0.5, wall, 1.0)

        def line(j, carry):
            base = n * 512 + j * 8
            even, odd = split([tile(f, base + 64 * i)[...] for i in range(8)])
            for p in pairs:
                slopes, bends = apply_d(even, odd, p), apply_k(even, odd, p)
                for i, slope, bend in zip((p, 7 - p), slopes, bends):
                    gone = tile(u, i * 64 + j * 8)[...] * slope + c0 * bend
                    tile(s, base + 64 * i)[...] = keep * (tile(s, base + 64 * i)[...] - gone)
            return carry

        lax.fori_loop(0, 8, line, 0, unroll=2)

    def join_span(ref, base):
        low, high = tile(ref, base), tile(ref, base + 56)
        shared = 0.5 * (low[...] + pltpu.roll(high[...], 1, 1))
        low[...] = shared
        high[...] = pltpu.roll(shared, 127, 1)

    def stage_faces(n):
        for j in range(8):
            spot = n * 64 + 8 * j
            tile(face_l, spot)[...] = oriented(tile(s, n * 512 + 8 * j)[...])
            tile(face_r, spot)[...] = tile(s, n * 512 + 448 + 8 * j)[...]

    def each(low, high, body):
        def run(n, carry):
            body(n)
            return carry

        lax.fori_loop(low, high, run, 0)

    near_out[0:8, :] = dec[...]
    near_out[8:16, :] = zero + flp[0].astype(F32)

    for i in (0, 7):
        start_plane(i)

    def velocity_faces(n):
        for i in (0, 7):
            step_plane(n, i)
        step_lines(n, (0,))
        for i in (0, 7):
            join_span(s, n * 512 + i * 64)
        stage_faces(n)

    each(0, 3, velocity_faces)

    pl.semaphore_wait(barrier, len(targets))
    faces = [
        send(face_l.at[0:192], got_r.at[0:192], face_send.at[0], face_recv.at[0], before),
        send(face_r.at[0:192], got_l.at[0:192], face_send.at[1], face_recv.at[1], after),
    ]
    nears = [
        send(near_out, near.at[0], near_send.at[0], near_recv.at[0], other_core),
        send(near_out, near.at[1], near_send.at[1], near_recv.at[1], outer),
        send(near_out, near.at[2], near_send.at[2], near_recv.at[2], outer_two),
    ]

    for p in (1, 2, 3):
        for i in (p, 7 - p):
            start_plane(i)

    def velocity_rest(n):
        def plane(i, carry):
            step_plane(n, i)
            return carry

        lax.fori_loop(1, 7, plane, 0)
        step_lines(n, (1, 2, 3))
        for i in range(1, 7):
            join_span(s, n * 512 + i * 64)

    each(0, 3, velocity_rest)

    def scalars(n):
        def plane(i, carry):
            step_plane(n, i)
            return carry

        lax.fori_loop(0, 8, plane, 0)
        step_lines(n, (0, 1, 2, 3))
        for i in range(8):
            join_span(s, n * 512 + i * 64)
        stage_faces(n)

    each(3, 5, scalars)
    faces += [
        send(face_l.at[192:320], got_r.at[192:320], face_send.at[2], face_recv.at[2], before),
        send(face_r.at[192:320], got_l.at[192:320], face_send.at[3], face_recv.at[3], after),
    ]

    across = msq[2] * by_row(COLUMN_SQ) + 1.0
    for a in range(4):
        for b in range(4):
            under = across + (float(COLUMN_SQ[a]) * msq[0] + float(COLUMN_SQ[b]) * msq[1])
            wgt[8 * (4 * a + b) : 8 * (4 * a + b) + 8, :] = 0.5 / under

    for copy in nears:
        copy.wait()
    own_a, partner_a, outer_a, far_a = dec[...], near[0, 0:8, :], near[1, 0:8, :], near[2, 0:8, :]
    first_core = zero + core.astype(F32) < 0.5
    not_start = 1.0 - at_start.astype(F32)
    not_end = 1.0 - at_end.astype(F32)
    a_0, a_1 = jnp.where(first_core, own_a, partner_a), jnp.where(first_core, partner_a, own_a)
    a_m, a_p = jnp.where(first_core, outer_a, far_a), jnp.where(first_core, far_a, outer_a)
    chip_first = (z * chips_n + chip == 0).astype(F32)
    chip_last = (z * chips_n + chip == nz * chips_n - 1).astype(F32)

    def root(a):
        return jnp.sqrt((1.0 - a) * (1.0 + a))

    s_0, s_1 = root(a_0), root(a_1)
    s_m, s_p = (1.0 - chip_first) * root(a_m), (1.0 - chip_last) * root(a_p)
    a_m, a_p = (1.0 - chip_first) * a_m, (1.0 - chip_last) * a_p
    ends_last = row < 4
    A_0, A_1 = jnp.where(ends_last, a_0, a_1), jnp.where(ends_last, a_1, a_p)
    R_0, R_1 = jnp.where(ends_last, a_m, a_0), jnp.where(ends_last, a_0, a_1)
    C_0 = jnp.where(ends_last, a_m * s_0 * a_0, s_0)
    C_1 = jnp.where(ends_last, a_0 * s_1 * a_1, s_1)
    s_own = jnp.where(first_core, s_0, s_1)
    a_before, s_before = jnp.where(first_core, a_m, a_0), jnp.where(first_core, s_m, s_0)
    a_after, s_after = jnp.where(first_core, a_1, a_p), jnp.where(first_core, s_1, s_p)
    k_1 = jnp.where(ends_last, s_own, a_after * s_own)
    k_2 = jnp.where(ends_last, own_a * s_before, s_after)
    k_3 = jnp.where(ends_last, a_before * s_own * s_own, s_own * s_own)
    k_4 = jnp.where(ends_last, a_before * s_own * k_2 + s_before * s_before, 0.0)
    flip_after = jnp.where(first_core, near[0, 8:16, :], near[1, 8:16, :]) == 1.0

    my_stat = stat.at[chip]
    my_stat[0] = A_0 * A_1
    my_stat[1] = R_0 * R_1
    my_stat[2] = C_0 + R_0 * C_1 * A_0
    for d in chip_order:
        send(my_stat, stat.at[chip], stat_sem.at[0], stat_sem.at[1], chip_peer(d))

    faces[0].wait()
    faces[1].wait()
    start_mask, end_mask = zero + not_start > 0.5, zero + not_end > 0.5

    def join_chain(n):
        for j in range(8):
            spot = n * 64 + 8 * j
            low, high = tile(s, n * 512 + 8 * j), tile(s, n * 512 + 448 + 8 * j)
            low[...] = jnp.where(start_mask, 0.5 * (low[...] + oriented(tile(got_l, spot)[...])), low[...])
            high[...] = jnp.where(end_mask, 0.5 * (high[...] + tile(got_r, spot)[...]), high[...])

    each(0, 3, join_chain)

    def divergence_plane(i):
        at_row = i * 64
        even, odd = split([strided(s, 1024 + at_row, k) for k in range(8)])
        for p in range(4):
            for k, slope in zip((p, 7 - p), apply_d(even, odd, p)):
                tt[8 * k : 8 * k + 8, :] = m[2] * slope
        even, odd = split([tile(s, 512 + at_row + 8 * j)[...] for j in range(8)])
        for p in range(4):
            for j, slope in zip((p, 7 - p), apply_d(even, odd, p)):
                tile(dv, at_row + 8 * j)[...] = m[1] * slope + strided(tt, 0, j)

    each(0, 8, divergence_plane)

    def guess_line(j):
        even, odd = split([tile(s, 64 * i + 8 * j)[...] for i in range(8)])
        nearer = jnp.minimum(j, 7 - j)
        for p in range(4):
            weight = tile(wgt, 8 * (4 * p + nearer))[...]
            for i, slope in zip((p, 7 - p), apply_d(even, odd, p)):
                spot = tile(dv, 64 * i + 8 * j)
                whole = spot[...] + m[0] * slope
                spot[...] = whole
                tile(fg, 64 * i + 8 * j)[...] = weight * whole

    each(0, 8, guess_line)

    def residual_plane(i):
        at_row = i * 64
        even, odd = split([strided(fg, at_row, k) for k in range(8)])
        for p in range(4):
            for k, bend in zip((p, 7 - p), apply_k(even, odd, p)):
                tt[8 * k : 8 * k + 8, :] = msq[2] * bend
        even, odd = split([tile(fg, at_row + 8 * j)[...] for j in range(8)])
        for p in range(4):
            for j, bend in zip((p, 7 - p), apply_k(even, odd, p)):
                at_j = at_row + 8 * j
                gone = tile(fg, at_j)[...] + msq[1] * bend + strided(tt, 0, j)
                tile(res, at_j)[...] = tile(dv, at_j)[...] - gone

    each(0, 8, residual_plane)

    def project_line(j):
        even, odd = split([tile(fg, 64 * i + 8 * j)[...] for i in range(8)])
        left = [None] * 8
        for p in range(4):
            for i, bend in zip((p, 7 - p), apply_k(even, odd, p)):
                left[i] = tile(res, 64 * i + 8 * j)[...] - msq[0] * bend
        low = high = None
        for i in range(1, 7):
            low = float(H[0, i]) * left[i] + (0.0 if low is None else low)
            high = float(H[1, i]) * left[i] + (0.0 if high is None else high)
        for n, part in enumerate((low, high, left[7], left[0])):
            tile(proj, n * 64 + 8 * j)[...] = part

    each(0, 8, project_line)

    gap = [by_row(H[0]), by_row(H[1])]
    sums = []
    for n in range(4):
        x = [proj[n * 64 + 8 * j : n * 64 + 8 * j + 8, :] for j in range(8)]
        shared = 0.5 * (x[0] + pltpu.roll(x[7], 1, 1))
        x[0], x[7] = shared, pltpu.roll(shared, 127, 1)
        modes = []
        for b in range(2):
            part = None
            for j in range(8):
                if H[b, j] != 0.0:
                    part = float(H[b, j]) * x[j] + (0.0 if part is None else part)
            for e in range(2):
                modes.append(jnp.sum(part * gap[e], axis=0, keepdims=True) * (1.0 / 64.0))
        sums.append(modes)

    def rows_of(values):
        out = zero
        for k, value in enumerate(values):
            out = jnp.where(row == k, value, out)
        return out

    inside = rows_of(sums[0] + sums[1])
    on_face = rows_of(sums[2] + sums[3])
    across_face = rows_of(sums[3] + sums[2])
    swapped = rows_of([part[e] for part in (sums[3], sums[2]) for e in (1, 0, 3, 2)])
    swap = jnp.where(ends_last, turned.astype(F32), flip_after.astype(F32)) > 0.5
    pushed = 0.5 * jnp.where(swap, swapped, across_face)
    own_share = jnp.where(ends_last, 1.0 - 0.5 * not_end, 1.0 - 0.5 * not_start)
    rhs = inside + own_share * on_face

    b_own = k_1 * rhs + k_2 * pushed
    d_own = k_3 * rhs + k_4 * pushed
    mine[0] = b_own
    mine[1] = d_own
    pair = send(mine, partner, pair_sem.at[0], pair_sem.at[1], other_core)
    pair.wait()
    B_0, D_0 = jnp.where(first_core, b_own, partner[0]), jnp.where(first_core, d_own, partner[1])
    B_1, D_1 = jnp.where(first_core, partner[0], b_own), jnp.where(first_core, partner[1], d_own)
    my_chip = chips.at[chip]
    my_chip[0] = A_1 * B_0 + B_1
    my_chip[1] = D_0 + R_0 * (C_1 * B_0 + D_1)
    for d in chip_order:
        send(my_chip, chips.at[chip], chip_sem.at[0], chip_sem.at[1], chip_peer(d))

    for i in range(8):
        join_span(fg, 64 * i)
    for j in range(8):
        tile(pface_l, 8 * j)[...] = oriented(tile(fg, 8 * j)[...])
        tile(pface_r, 8 * j)[...] = tile(fg, 448 + 8 * j)[...]
    pfaces = [
        send(pface_l, pgot_r, pface_send.at[0], pface_recv.at[0], before),
        send(pface_r, pgot_l, pface_send.at[1], pface_recv.at[1], after),
    ]
    faces[2].wait()
    faces[3].wait()
    each(3, 5, join_chain)
    adv_copy = pltpu.make_async_copy(s, adv_out, out_sem.at[0])
    adv_copy.start()

    wait_bytes(stat.at[0 : chips_n - 1], stat_sem.at[1])
    wait_bytes(stat.at[0 : chips_n - 1], stat_sem.at[0])

    def factors_up(n, up):
        pre[n, 0] = up
        return stat[n, 0] * up

    ones = zero + 1.0
    slab_a = lax.fori_loop(0, chips_n, factors_up, ones, unroll=4)

    def factors_down(t, carry):
        n = chips_n - 1 - t
        down, mixed = carry
        pre[n, 1] = down
        pre[n, 2] = mixed
        return stat[n, 1] * down, stat[n, 1] * mixed + stat[n, 2] * pre[n, 0]

    slab_r, slab_c = lax.fori_loop(0, chips_n, factors_down, (ones, zero), unroll=4)
    my_zstat = zstat.at[z]
    my_zstat[0] = slab_a
    my_zstat[1] = slab_r
    my_zstat[2] = slab_c
    for d in slab_order:
        send(my_zstat, zstat.at[z], zstat_sem.at[0], zstat_sem.at[1], slab_peer(d))

    for copy in pfaces:
        copy.wait()
    for j in range(8):
        low, high = tile(fg, 8 * j), tile(fg, 448 + 8 * j)
        low[...] = jnp.where(start_mask, 0.5 * (low[...] + oriented(tile(pgot_l, 8 * j)[...])), low[...])
        high[...] = jnp.where(end_mask, 0.5 * (high[...] + tile(pgot_r, 8 * j)[...]), high[...])

    wait_bytes(chips.at[0 : chips_n - 1], chip_sem.at[1])

    def chips_up(n, up):
        pre[n, 3] = up
        return stat[n, 0] * up + chips[n, 0]

    slab_b = lax.fori_loop(0, chips_n, chips_up, zero, unroll=4)

    def chips_down(t, down):
        n = chips_n - 1 - t
        pre[n, 4] = down
        return stat[n, 1] * down + (stat[n, 2] * pre[n, 3] + chips[n, 1])

    slab_d = lax.fori_loop(0, chips_n, chips_down, zero, unroll=4)
    my_slab = slabs.at[z]
    my_slab[0] = slab_b
    my_slab[1] = slab_d
    for d in slab_order:
        send(my_slab, slabs.at[z], slab_sem.at[0], slab_sem.at[1], slab_peer(d))

    wait_bytes(chips.at[0 : chips_n - 1], chip_sem.at[0])
    wait_bytes(zstat.at[0 : nz - 1], zstat_sem.at[0])
    wait_bytes(zstat.at[0 : nz - 1], zstat_sem.at[1])
    wait_bytes(slabs.at[0 : nz - 1], slab_sem.at[1])

    up, down = zero, zero
    for n in range(nz):
        kept[n, 0] = up
        up = zstat[n, 0] * up + slabs[n, 0]
    for n in range(nz - 1, -1, -1):
        kept[n, 1] = down
        down = zstat[n, 1] * down + (zstat[n, 2] * kept[n, 0] + slabs[n, 1])
    up, down = kept[z, 0], kept[z, 1]
    chip_up = pre[chip, 3] + pre[chip, 0] * up
    chip_down = pre[chip, 4] + pre[chip, 1] * down + pre[chip, 2] * up
    middle = A_0 * chip_up + B_0
    up = jnp.where(first_core, chip_up, middle)
    down = jnp.where(first_core, R_1 * chip_down + C_1 * middle + D_1, chip_down)
    back = jnp.where(
        ends_last, down + s_own * (own_a * up + b_own), own_a * down + s_own * (up + s_own * rhs)
    )

    modes = [jnp.broadcast_to(back[k : k + 1, :], (8, 128)) for k in range(8)]
    edges = [gap[0] * modes[2 * k] + gap[1] * modes[2 * k + 1] for k in range(4)]
    for j in range(8):
        ends = [float(H[0, j]) * edges[2 * a] + float(H[1, j]) * edges[2 * a + 1] for a in range(2)]
        for i in range(8):
            spot = tile(fg, 64 * i + 8 * j)
            spot[...] = spot[...] + float(H[0, i]) * ends[0] + float(H[1, i]) * ends[1]
    prs_copy = pltpu.make_async_copy(fg, prs_out, out_sem.at[1])
    prs_copy.start()
    wait_bytes(slabs.at[0 : nz - 1], slab_sem.at[0])
    adv_copy.wait()
    prs_copy.wait()


def solution(mesh):
    nz, sub_n = mesh.shape["slab"], mesh.shape["sub"]
    nx = 2 if sub_n == 8 else 4
    ny = sub_n // (2 * nx)
    vmem = lambda *shape: pltpu.VMEM(shape, F32)
    dma = lambda n: pltpu.SemaphoreType.DMA((n,))
    anywhere = pl.BlockSpec(memory_space=pl.ANY)

    def local(fields, metric, diffusivity, joule_heat, face_flip, coarse_decay):
        advanced, pressure = pl.pallas_call(
            functools.partial(kernel, (nz, nx, ny)),
            name="step",
            out_shape=(jax.ShapeDtypeStruct((2560, 128), F32), jax.ShapeDtypeStruct((512, 128), F32)),
            in_specs=[anywhere] * 6,
            out_specs=(anywhere, anywhere),
            scratch_shapes=[
                vmem(2560, 128),
                vmem(512, 128),
                vmem(3, 1, 128),
                pltpu.SMEM((5,), F32),
                pltpu.SMEM((1,), jnp.int32),
                vmem(8, 128),
                vmem(2560, 128),
                vmem(1536, 128),
                vmem(64, 128),
                vmem(512, 128),
                vmem(512, 128),
                vmem(512, 128),
                vmem(128, 128),
                vmem(256, 128),
                vmem(nz, 2, 8, 128),
                vmem(320, 128),
                vmem(320, 128),
                vmem(320, 128),
                vmem(320, 128),
                vmem(64, 128),
                vmem(64, 128),
                vmem(64, 128),
                vmem(64, 128),
                vmem(16, 128),
                vmem(3, 16, 128),
                vmem(2, 8, 128),
                vmem(2, 8, 128),
                vmem(nx * ny, 2, 8, 128),
                vmem(nx * ny, 3, 8, 128),
                vmem(nx * ny, 5, 8, 128),
                vmem(nz, 2, 8, 128),
                vmem(nz, 3, 8, 128),
                dma(6), dma(2), dma(4), dma(4), dma(2), dma(2), dma(3), dma(3),
                dma(2), dma(2), dma(2), dma(2), dma(2),
            ],
            compiler_params=pltpu.CompilerParams(
                collective_id=0, has_side_effects=True, vmem_limit_bytes=32 * 1024 * 1024
            ),
        )(
            fields.reshape(2560, 128), joule_heat.reshape(512, 128), metric, diffusivity,
            face_flip, coarse_decay.reshape(8, 128),
        )
        return advanced.reshape(5, 512, 1, 128), pressure.reshape(512, 1, 128)

    in_specs = (
        P(None, None, ("slab", "sub"), None),
        P(None, ("slab", "sub"), None),
        P(),
        P(None, ("slab", "sub"), None),
        P(("slab", "sub")),
        P(None, ("slab", "sub"), None),
    )
    out_specs = (P(None, None, ("slab", "sub"), None), P(None, ("slab", "sub"), None))
    return jax.shard_map(local, mesh=mesh, in_specs=in_specs, out_specs=out_specs, check_vma=False)
```

time: 530 us -> 56.2 us (0.11)
  the two profiles are of different devices: /device:TPU:64 before, /device:TPU:1 now
where the time goes in v1:
time: 56.2 us; the launch traced here: 55.9 us
  Pallas kernels  48.6 us (86%)
  local copies, waits for them, and re-layouts  6.04 us (11%)
  between operations  1.3 us (2%)
    pallas_call x1, Pallas kernels, local(): pl.pallas_call(functools.partial(kernel, (nz, nx, ny)), name='step', out_...  48.6 us
    unnamed x12, local copies, waits for them, and re-layouts  6.04 us

profile of v1, /device:TPU:1, one launch (start us, length us, event | category | flops | bytes accessed | tf_op | source)
XLA Modules:
  0.0 55.9 jit_solution(2020602538822804955)
XLA Ops:
  1.3 0.0 copy-start
  1.3 1.3 %copy-done = f32[5,512,1,128]{3,2,1,0:T(1,128)S(1)} copy-done((f32[5,512,1,128]{3,2,1,0:T(1,128)S(1)}, f32[5,512,1,128]{3,2,1,0:T(1,128)}, u32[]{:S(2)}) %copy-start) | copy-done | bytes 1310744
  2.6 0.0 copy-start.1
  2.6 0.9 %copy-done.1 = f32[512,1,128]{2,1,0:T(1,128)S(1)} copy-done((f32[512,1,128]{2,1,0:T(1,128)S(1)}, f32[512,1,128]{2,1,0:T(1,128)}, u32[]{:S(2)}) %copy-start.1) | copy-done | bytes 262168
  3.5 0.0 copy-start.2
  3.5 0.7 %copy-done.2 = f32[8,1,128]{2,1,0:T(1,128)S(1)} copy-done((f32[8,1,128]{2,1,0:T(1,128)S(1)}, f32[8,1,128]{2,1,0:T(1,128)}, u32[]{:S(2)}) %copy-start.2) | copy-done | bytes 4120
  4.2 0.0 copy-start.3
  4.2 0.7 %copy-done.3 = f32[3,1,128]{2,1,0:T(1,128)S(1)} copy-done((f32[3,1,128]{2,1,0:T(1,128)S(1)}, f32[3,1,128]{2,1,0:T(1,128)}, u32[]{:S(2)}) %copy-start.3) | copy-done | bytes 1560
  4.9 0.0 copy-start.4
  4.9 0.7 %copy-done.4 = f32[5]{0:T(128)S(1)} copy-done((f32[5]{0:T(128)S(1)}, f32[5]{0:T(128)}, u32[]{:S(2)}) %copy-start.4) | copy-done | bytes 44
  5.6 48.6 %step.1 = (f32[2560,128]{1,0:T(8,128)S(1)}, f32[512,128]{1,0:T(8,128)S(1)}) custom-call(f32[2560,128]{1,0:T(8,128)S(1)} %bitcast.9, f32[512,128]{1,0:T(8,128)S(1)} %bitcast.12, f32[3,1,128]{2,1,0:T(1,128)S(1)} %copy-done.3, f32[5]{0:T(128)S(1)} %copy-done.4, s32[1]{0:T(128)S(6)} %copy.12.flip, f32[8,128]{1,0:T(8,128)S(1)} %bitcast.13), custom_call_target="tpu_custom_call" | custom-call | tf_op jit(solution)/shard_map/step/pallas_call | solution.py:562
  54.1 1.1 %copy.13 = f32[5,512,1,128]{3,2,1,0:T(1,128)} copy(f32[5,512,1,128]{3,2,1,0:T(1,128)S(1)} %bitcast.10) | data formatting | bytes 2621440
  55.2 0.7 %copy.14 = f32[512,1,128]{2,1,0:T(1,128)} copy(f32[512,1,128]{2,1,0:T(1,128)S(1)} %bitcast.11) | data formatting | bytes 524288
Async XLA Ops:
  1.3 1.3 %copy-start = (f32[5,512,1,128]{3,2,1,0:T(1,128)S(1)}, f32[5,512,1,128]{3,2,1,0:T(1,128)}, u32[]{:S(2)}) copy-start(f32[5,512,1,128]{3,2,1,0:T(1,128)} %param.6) | copy-start | bytes 3932164
  2.6 0.9 %copy-start.1 = (f32[512,1,128]{2,1,0:T(1,128)S(1)}, f32[512,1,128]{2,1,0:T(1,128)}, u32[]{:S(2)}) copy-start(f32[512,1,128]{2,1,0:T(1,128)} %param.9) | copy-start | bytes 786436
  3.5 0.7 %copy-start.2 = (f32[8,1,128]{2,1,0:T(1,128)S(1)}, f32[8,1,128]{2,1,0:T(1,128)}, u32[]{:S(2)}) copy-start(f32[8,1,128]{2,1,0:T(1,128)} %param.11) | copy-start | bytes 12292
  4.2 0.7 %copy-start.3 = (f32[3,1,128]{2,1,0:T(1,128)S(1)}, f32[3,1,128]{2,1,0:T(1,128)}, u32[]{:S(2)}) copy-start(f32[3,1,128]{2,1,0:T(1,128)} %metric.1) | copy-start | bytes 4612
  4.9 0.7 %copy-start.4 = (f32[5]{0:T(128)S(1)}, f32[5]{0:T(128)}, u32[]{:S(2)}) copy-start(f32[5]{0:T(128)} %diffusivity.1) | copy-start | bytes 64

commit v2 on v1

--- a/solution.py
+++ b/solution.py
@@ -65,12 +65,14 @@
 
 
 def kernel(
-    sizes, fields, heat, metric, diffusivity, flip, decay, adv_out, prs_out,
-    f, q, met, dif, flp, dec, s, u, tt, dv, fg, res, wgt, proj, kept,
+    sizes, fields, heat, metric, diffusivity, flip, decay, adv_out, guess_out, back_out,
+    f, q, met, dif, flp, dec, s, u, tt, dv, fg, res, wgt, proj,
     face_l, face_r, got_l, got_r, pface_l, pface_r, pgot_l, pgot_r,
-    near_out, near, mine, partner, chips, stat, pre, slabs, zstat,
+    near_out, near, mine, partner, rates, edge, backs,
+    y_stat, y_push, y_pre, x_stat, x_push, x_pre, z_stat, z_push, z_pre,
     load_sem, out_sem, face_send, face_recv, pface_send, pface_recv, near_send, near_recv,
-    pair_sem, chip_sem, stat_sem, slab_sem, zstat_sem,
+    pair_sem, rate_sem, swap_sem, edge_send, edge_recv, push_send, push_recv, stat_send, stat_recv,
+    stat_tail_send, stat_tail_recv, push_tail_send, push_tail_recv, heard,
 ):
     nz, nx, ny = sizes
     chips_n = nx * ny
@@ -91,23 +93,50 @@
     other_core = (z, sub - side)
     before, after = at(here - 1), at(here + 1)
     outer, outer_two, inner_two = at(here + side), at(here + 2 * side), at(here - 2 * side)
-    chip_order = sorted(range(1, chips_n), key=lambda d: -(ring(nx, d // ny) + ring(ny, d % ny)))
-    slab_order = sorted(range(1, nz), key=lambda d: -ring(nz, d))
-
-    def chip_peer(d):
-        px, py = lax.rem(cx + d // ny, nx), lax.rem(cy + d % ny, ny)
-        return (z, (px * ny + py) * 2 + core)
-
-    def slab_peer(d):
-        return (lax.rem(z + d, nz), sub)
-
-    def send(src, dst, send_sem, recv_sem, device):
-        copy = pltpu.make_async_remote_copy(
+    chip_at = z * chips_n + chip
+    more_before, more_after = chip_at > 0, chip_at < nz * chips_n - 1
+    has_outer = jnp.where(core == 0, more_before, more_after)
+    has_inner = jnp.where(core == 0, more_after, more_before)
+    by_distance = lambda n: sorted(range(1, n), key=lambda d: -ring(n, d))
+    y_order, x_order, z_order = by_distance(ny), by_distance(nx), by_distance(nz)
+
+    def shift(dx, dy, dz):
+        px, py = lax.rem(cx + dx + nx, nx), lax.rem(cy + dy + ny, ny)
+        return (lax.rem(z + dz + nz, nz), (px * ny + py) * 2 + core)
+
+    y_peers = [shift(0, d, 0) for d in y_order]
+    x_peers = [shift(d, 0, 0) for d in x_order]
+    z_peers = [shift(0, 0, d) for d in z_order]
+
+    def remote(src, dst, send_sem, recv_sem, device):
+        return pltpu.make_async_remote_copy(
             src_ref=src, dst_ref=dst, send_sem=send_sem, recv_sem=recv_sem,
             device_id=device, device_id_type=MESH,
         )
+
+    def send(*args):
+        copy = remote(*args)
         copy.start()
         return copy
+
+    def when(condition, action):
+        if condition is None:
+            action()
+        else:
+            pl.when(condition)(action)
+
+    class Exchange:
+        def __init__(self, parts):
+            self.parts = [(sent, got, remote(*args)) for sent, got, args in parts]
+
+        def start(self):
+            for sent, _, copy in self.parts:
+                when(sent, copy.start)
+
+        def wait(self):
+            for sent, got, copy in self.parts:
+                when(got, copy.wait_recv)
+                when(sent, copy.wait_send)
 
     def wait_bytes(ref, sem):
         pltpu.make_async_copy(ref, ref, sem).wait()
@@ -117,17 +146,37 @@
         pltpu.make_async_copy(metric, met, load_sem.at[1]),
         pltpu.make_async_copy(flip, flp, load_sem.at[2]),
         pltpu.make_async_copy(diffusivity, dif, load_sem.at[3]),
-        pltpu.make_async_copy(fields, f, load_sem.at[4]),
-        pltpu.make_async_copy(heat, q, load_sem.at[5]),
+        pltpu.make_async_copy(heat, q, load_sem.at[4]),
     ]
+    for n in range(5):
+        spot = pl.ds(512 * n, 512)
+        loads.append(pltpu.make_async_copy(fields.at[spot], f.at[spot], load_sem.at[5 + n]))
     for copy in loads:
         copy.start()
 
+    def offsets(n, wanted):
+        return sorted({d % n for d in wanted} - {0})
+
+    near_x = offsets(nx, (1, 2, 3))
+    near_y = offsets(ny, (1, 2, -1, -2))
+    near_z = offsets(nz, (1, 2, -1, -2))
     barrier = pltpu.get_barrier_semaphore()
-    targets = [other_core, outer, inner_two]
-    targets += [chip_peer(d) for d in chip_order] + [slab_peer(d) for d in slab_order]
+    targets = [other_core] + [shift(d, 0, 0) for d in near_x]
+    targets += [shift(0, d, 0) for d in near_y] + [shift(0, 0, d) for d in near_z]
     for device in targets:
         pl.semaphore_signal(barrier, inc=1, device_id=device, device_id_type=MESH)
+    for condition, device in ((has_outer, outer), (has_inner, inner_two)):
+
+        @pl.when(condition)
+        def _():
+            pl.semaphore_signal(barrier, inc=1, device_id=device, device_id_type=MESH)
+
+    second = [shift(0, d, 0) for d in offsets(ny, (2, -2))] + [shift(0, 0, d) for d in offsets(nz, (2, -2))]
+    third = [shift(0, 0, d) for d in offsets(nz, (4, -4))]
+
+    def pass_word(k, devices):
+        for device in devices:
+            pl.semaphore_signal(heard.at[k], inc=1, device_id=device, device_id_type=MESH)
 
     for copy in loads:
         copy.wait()
@@ -243,18 +292,36 @@
             join_span(s, n * 512 + i * 64)
         stage_faces(n)
 
-    each(0, 3, velocity_faces)
-
-    pl.semaphore_wait(barrier, len(targets))
-    faces = [
-        send(face_l.at[0:192], got_r.at[0:192], face_send.at[0], face_recv.at[0], before),
-        send(face_r.at[0:192], got_l.at[0:192], face_send.at[1], face_recv.at[1], after),
-    ]
-    nears = [
-        send(near_out, near.at[0], near_send.at[0], near_recv.at[0], other_core),
-        send(near_out, near.at[1], near_send.at[1], near_recv.at[1], outer),
-        send(near_out, near.at[2], near_send.at[2], near_recv.at[2], outer_two),
-    ]
+    each(0, 2, velocity_faces)
+
+    pl.semaphore_wait(barrier, len(targets) + 2 * has_outer.astype(jnp.int32))
+    pass_word(0, second)
+    nears = Exchange([
+        (None, None, (near_out, near.at[0], near_send.at[0], near_recv.at[0], other_core)),
+        (has_outer, has_outer, (near_out, near.at[1], near_send.at[1], near_recv.at[1], outer)),
+        (has_outer, has_inner, (near_out, near.at[2], near_send.at[2], near_recv.at[2], outer_two)),
+    ])
+    nears.start()
+    for condition, k in ((has_outer, 1), (has_inner, 2)):
+
+        @pl.when(jnp.logical_not(condition))
+        def _():
+            near[k] = jnp.zeros((16, 128), F32)
+
+    each(2, 3, velocity_faces)
+
+    def chain_exchange(left, right, from_left, from_right, sems, k):
+        ahead, behind = jnp.logical_not(at_end), jnp.logical_not(at_start)
+        return Exchange([
+            (behind, ahead, (left, from_right, sems[0].at[k], sems[1].at[k], before)),
+            (ahead, behind, (right, from_left, sems[0].at[k + 1], sems[1].at[k + 1], after)),
+        ])
+
+    part = slice(0, 192)
+    velocity_exchange = chain_exchange(
+        face_l.at[part], face_r.at[part], got_l.at[part], got_r.at[part], (face_send, face_recv), 0
+    )
+    velocity_exchange.start()
 
     for p in (1, 2, 3):
         for i in (p, 7 - p):
@@ -270,24 +337,13 @@
         for i in range(1, 7):
             join_span(s, n * 512 + i * 64)
 
-    each(0, 3, velocity_rest)
-
-    def scalars(n):
-        def plane(i, carry):
-            step_plane(n, i)
-            return carry
-
-        lax.fori_loop(0, 8, plane, 0)
-        step_lines(n, (0, 1, 2, 3))
-        for i in range(8):
-            join_span(s, n * 512 + i * 64)
-        stage_faces(n)
-
-    each(3, 5, scalars)
-    faces += [
-        send(face_l.at[192:320], got_r.at[192:320], face_send.at[2], face_recv.at[2], before),
-        send(face_r.at[192:320], got_l.at[192:320], face_send.at[3], face_recv.at[3], after),
-    ]
+    each(0, 2, velocity_rest)
+    pl.semaphore_wait(heard.at[0], len(second))
+    pass_word(1, third)
+    rates[core, cy + 1] = dec[...]
+    for device in y_peers:
+        send(dec, rates.at[core, cy + 1], rate_sem.at[0], rate_sem.at[1], device)
+    each(2, 3, velocity_rest)
 
     across = msq[2] * by_row(COLUMN_SQ) + 1.0
     for a in range(4):
@@ -295,8 +351,7 @@
             under = across + (float(COLUMN_SQ[a]) * msq[0] + float(COLUMN_SQ[b]) * msq[1])
             wgt[8 * (4 * a + b) : 8 * (4 * a + b) + 8, :] = 0.5 / under
 
-    for copy in nears:
-        copy.wait()
+    nears.wait()
     own_a, partner_a, outer_a, far_a = dec[...], near[0, 0:8, :], near[1, 0:8, :], near[2, 0:8, :]
     first_core = zero + core.astype(F32) < 0.5
     not_start = 1.0 - at_start.astype(F32)
@@ -312,10 +367,21 @@
     s_0, s_1 = root(a_0), root(a_1)
     s_m, s_p = (1.0 - chip_first) * root(a_m), (1.0 - chip_last) * root(a_p)
     a_m, a_p = (1.0 - chip_first) * a_m, (1.0 - chip_last) * a_p
+
+    edge[0] = a_m
+    edge[1] = a_p
+    ends = ((cy == 0, 0, (1, 0)), (cy == ny - 1, 1, (0, ny + 1)))
+    for is_end, k, place in ends:
+
+        @pl.when(is_end)
+        def _():
+            rates[place] = edge[k]
+            for device in y_peers:
+                send(edge.at[k], rates.at[place], edge_send.at[k], edge_recv.at[k], device)
+
     ends_last = row < 4
     A_0, A_1 = jnp.where(ends_last, a_0, a_1), jnp.where(ends_last, a_1, a_p)
     R_0, R_1 = jnp.where(ends_last, a_m, a_0), jnp.where(ends_last, a_0, a_1)
-    C_0 = jnp.where(ends_last, a_m * s_0 * a_0, s_0)
     C_1 = jnp.where(ends_last, a_0 * s_1 * a_1, s_1)
     s_own = jnp.where(first_core, s_0, s_1)
     a_before, s_before = jnp.where(first_core, a_m, a_0), jnp.where(first_core, s_m, s_0)
@@ -326,15 +392,7 @@
     k_4 = jnp.where(ends_last, a_before * s_own * k_2 + s_before * s_before, 0.0)
     flip_after = jnp.where(first_core, near[0, 8:16, :], near[1, 8:16, :]) == 1.0
 
-    my_stat = stat.at[chip]
-    my_stat[0] = A_0 * A_1
-    my_stat[1] = R_0 * R_1
-    my_stat[2] = C_0 + R_0 * C_1 * A_0
-    for d in chip_order:
-        send(my_stat, stat.at[chip], stat_sem.at[0], stat_sem.at[1], chip_peer(d))
-
-    faces[0].wait()
-    faces[1].wait()
+    velocity_exchange.wait()
     start_mask, end_mask = zero + not_start > 0.5, zero + not_end > 0.5
 
     def join_chain(n):
@@ -441,94 +499,181 @@
     pair.wait()
     B_0, D_0 = jnp.where(first_core, b_own, partner[0]), jnp.where(first_core, d_own, partner[1])
     B_1, D_1 = jnp.where(first_core, partner[0], b_own), jnp.where(first_core, partner[1], d_own)
-    my_chip = chips.at[chip]
-    my_chip[0] = A_1 * B_0 + B_1
-    my_chip[1] = D_0 + R_0 * (C_1 * B_0 + D_1)
-    for d in chip_order:
-        send(my_chip, chips.at[chip], chip_sem.at[0], chip_sem.at[1], chip_peer(d))
-
+    y_push[cy, 0] = A_1 * B_0 + B_1
+    y_push[cy, 1] = D_0 + R_0 * (C_1 * B_0 + D_1)
+
+    def spread(ref, place, k, sems, devices):
+        for device in devices:
+            send(ref.at[place], ref.at[place], sems[0].at[k], sems[1].at[k], device)
+
+    def spread_ended(ref, k, sem, devices):
+        wait_bytes(ref.at[0 : len(devices)], sem.at[k])
+
+    pushes, stats = (push_send, push_recv), (stat_send, stat_recv)
+    def spread_z(ref, first, sems, k, tail_sems):
+        rest = pl.ds(first, ref.shape[1] - first)
+        for d, device in zip(z_order, z_peers):
+            head = ref.at[z, pl.ds(0, first)]
+            send(head, head, sems[0].at[k], sems[1].at[k], device)
+
+            @pl.when(z + d >= nz)
+            def _():
+                tail = ref.at[z, rest]
+                send(tail, tail, tail_sems[0].at[d], tail_sems[1].at[z], device)
+
+    def spread_z_got(ref, first, sem, k, tail_sem):
+        rest = pl.ds(first, ref.shape[1] - first)
+        wait_bytes(ref.at[0 : nz - 1, pl.ds(0, first)], sem.at[k])
+        for n in range(1, nz):
+
+            @pl.when(z < n)
+            def _():
+                wait_bytes(ref.at[n, rest], tail_sem.at[n])
+
+    def spread_z_left(ref, first, sem, k, tail_sem):
+        rest = pl.ds(first, ref.shape[1] - first)
+        wait_bytes(ref.at[0 : nz - 1, pl.ds(0, first)], sem.at[k])
+        for d in range(1, nz):
+
+            @pl.when(z + d >= nz)
+            def _():
+                wait_bytes(ref.at[z, rest], tail_sem.at[d])
+
+    z_stat_tail, z_push_tail = (stat_tail_send, stat_tail_recv), (push_tail_send, push_tail_recv)
+    spread(y_push, cy, 0, pushes, y_peers)
+
+    wait_bytes(rates.at[core, pl.ds(1, ny - 1)], rate_sem.at[1])
+    half = rates.at[core, pl.ds(1, ny)]
+    swap_halves = send(half, half, swap_sem.at[0], swap_sem.at[1], other_core)
+    for is_end, k, place in ends:
+
+        @pl.when(jnp.logical_not(is_end))
+        def _():
+            wait_bytes(rates.at[place], edge_recv.at[k])
+
+    swap_halves.wait()
+
+    roots = [[root(rates[c, n + 1]) for n in range(ny)] for c in range(2)]
+    for n in range(ny):
+        e_m, e_0 = rates[1, n], rates[0, n + 1]
+        e_1, e_p = rates[1, n + 1], rates[0, n + 2]
+        both, lead = e_0 * e_1, e_m * e_0
+        mixed = roots[0][n] + both * roots[1][n]
+        y_stat[n, 0] = jnp.where(ends_last, both, e_1 * e_p)
+        y_stat[n, 1] = jnp.where(ends_last, lead, both)
+        y_stat[n, 2] = jnp.where(ends_last, lead * mixed, mixed)
+
+    ones = zero + 1.0
+
+    def combine_stat(stat, pre, count):
+        up = ones
+        for n in range(count):
+            pre[n, 0] = up
+            up = stat[n, 0] * up
+        down, mixed = ones, zero
+        for n in range(count - 1, -1, -1):
+            pre[n, 1] = down
+            pre[n, 2] = mixed
+            mixed = stat[n, 1] * mixed + stat[n, 2] * pre[n, 0]
+            down = stat[n, 1] * down
+        return up, down, mixed
+
+    def combine_push(stat, push, pre, count):
+        up = zero
+        for n in range(count):
+            pre[n, 3] = up
+            up = stat[n, 0] * up + push[n, 0]
+        down = zero
+        for n in range(count - 1, -1, -1):
+            pre[n, 4] = down
+            down = stat[n, 1] * down + (stat[n, 2] * pre[n, 3] + push[n, 1])
+        return up, down
+
+    def set_stat(ref, place, values):
+        for k, value in enumerate(values):
+            ref[place, k] = value
+
+    set_stat(x_stat, cx, combine_stat(y_stat, y_pre, ny))
+    spread(x_stat, cx, 0, stats, x_peers)
+
+    def scalars(n):
+        def plane(i, carry):
+            step_plane(n, i)
+            return carry
+
+        lax.fori_loop(0, 8, plane, 0)
+        step_lines(n, (0, 1, 2, 3))
+        for i in range(8):
+            join_span(s, n * 512 + i * 64)
+        stage_faces(n)
+
+    each(3, 5, scalars)
     for i in range(8):
         join_span(fg, 64 * i)
     for j in range(8):
         tile(pface_l, 8 * j)[...] = oriented(tile(fg, 8 * j)[...])
         tile(pface_r, 8 * j)[...] = tile(fg, 448 + 8 * j)[...]
-    pfaces = [
-        send(pface_l, pgot_r, pface_send.at[0], pface_recv.at[0], before),
-        send(pface_r, pgot_l, pface_send.at[1], pface_recv.at[1], after),
-    ]
-    faces[2].wait()
-    faces[3].wait()
-    each(3, 5, join_chain)
-    adv_copy = pltpu.make_async_copy(s, adv_out, out_sem.at[0])
-    adv_copy.start()
-
-    wait_bytes(stat.at[0 : chips_n - 1], stat_sem.at[1])
-    wait_bytes(stat.at[0 : chips_n - 1], stat_sem.at[0])
-
-    def factors_up(n, up):
-        pre[n, 0] = up
-        return stat[n, 0] * up
-
-    ones = zero + 1.0
-    slab_a = lax.fori_loop(0, chips_n, factors_up, ones, unroll=4)
-
-    def factors_down(t, carry):
-        n = chips_n - 1 - t
-        down, mixed = carry
-        pre[n, 1] = down
-        pre[n, 2] = mixed
-        return stat[n, 1] * down, stat[n, 1] * mixed + stat[n, 2] * pre[n, 0]
-
-    slab_r, slab_c = lax.fori_loop(0, chips_n, factors_down, (ones, zero), unroll=4)
-    my_zstat = zstat.at[z]
-    my_zstat[0] = slab_a
-    my_zstat[1] = slab_r
-    my_zstat[2] = slab_c
-    for d in slab_order:
-        send(my_zstat, zstat.at[z], zstat_sem.at[0], zstat_sem.at[1], slab_peer(d))
-
-    for copy in pfaces:
-        copy.wait()
+
+    pl.semaphore_wait(heard.at[1], len(third)) if third else None
+    spread_ended(x_stat, 0, stat_recv, x_peers)
+    set_stat(z_stat, z, combine_stat(x_stat, x_pre, nx))
+    spread_z(z_stat, 1, stats, 1, z_stat_tail)
+
+    spread_ended(y_push, 0, push_recv, y_peers)
+    set_stat(x_push, cx, combine_push(y_stat, y_push, y_pre, ny))
+    spread(x_push, cx, 1, pushes, x_peers)
+    guess_exchange = chain_exchange(pface_l, pface_r, pgot_l, pgot_r, (pface_send, pface_recv), 0)
+    guess_exchange.start()
+    part = slice(192, 320)
+    scalar_exchange = chain_exchange(
+        face_l.at[part], face_r.at[part], got_l.at[part], got_r.at[part], (face_send, face_recv), 2
+    )
+    scalar_exchange.start()
+    spread_ended(x_push, 1, push_recv, x_peers)
+    set_stat(z_push, z, combine_push(x_stat, x_push, x_pre, nx))
+    spread_z(z_push, 1, pushes, 2, z_push_tail)
+    wait_bytes(rates.at[core, pl.ds(1, ny - 1)], rate_sem.at[0])
+    spread_ended(y_push, 0, push_send, y_peers)
+    spread_ended(x_stat, 0, stat_send, x_peers)
+    spread_ended(x_push, 1, push_send, x_peers)
+    for is_end, k, place in ends:
+
+        @pl.when(is_end)
+        def _():
+            wait_bytes(rates.at[0, pl.ds(1, ny - 1)], edge_send.at[k])
+
+    guess_exchange.wait()
     for j in range(8):
         low, high = tile(fg, 8 * j), tile(fg, 448 + 8 * j)
         low[...] = jnp.where(start_mask, 0.5 * (low[...] + oriented(tile(pgot_l, 8 * j)[...])), low[...])
         high[...] = jnp.where(end_mask, 0.5 * (high[...] + tile(pgot_r, 8 * j)[...]), high[...])
-
-    wait_bytes(chips.at[0 : chips_n - 1], chip_sem.at[1])
-
-    def chips_up(n, up):
-        pre[n, 3] = up
-        return stat[n, 0] * up + chips[n, 0]
-
-    slab_b = lax.fori_loop(0, chips_n, chips_up, zero, unroll=4)
-
-    def chips_down(t, down):
-        n = chips_n - 1 - t
-        pre[n, 4] = down
-        return stat[n, 1] * down + (stat[n, 2] * pre[n, 3] + chips[n, 1])
-
-    slab_d = lax.fori_loop(0, chips_n, chips_down, zero, unroll=4)
-    my_slab = slabs.at[z]
-    my_slab[0] = slab_b
-    my_slab[1] = slab_d
-    for d in slab_order:
-        send(my_slab, slabs.at[z], slab_sem.at[0], slab_sem.at[1], slab_peer(d))
-
-    wait_bytes(chips.at[0 : chips_n - 1], chip_sem.at[0])
-    wait_bytes(zstat.at[0 : nz - 1], zstat_sem.at[0])
-    wait_bytes(zstat.at[0 : nz - 1], zstat_sem.at[1])
-    wait_bytes(slabs.at[0 : nz - 1], slab_sem.at[1])
-
-    up, down = zero, zero
+    scalar_exchange.wait()
+    each(3, 5, join_chain)
+    adv_copy = pltpu.make_async_copy(s, adv_out, out_sem.at[0])
+    adv_copy.start()
+
+    guess_copy = pltpu.make_async_copy(fg, guess_out, out_sem.at[1])
+    guess_copy.start()
+
+    spread_z_got(z_stat, 1, stat_recv, 1, stat_tail_recv)
+    spread_z_got(z_push, 1, push_recv, 2, push_tail_recv)
+
+    up = zero
     for n in range(nz):
-        kept[n, 0] = up
-        up = zstat[n, 0] * up + slabs[n, 0]
+        z_pre[n, 3] = up
+        up = z_stat[n, 0] * up + z_push[n, 0]
+    down = zero
     for n in range(nz - 1, -1, -1):
-        kept[n, 1] = down
-        down = zstat[n, 1] * down + (zstat[n, 2] * kept[n, 0] + slabs[n, 1])
-    up, down = kept[z, 0], kept[z, 1]
-    chip_up = pre[chip, 3] + pre[chip, 0] * up
-    chip_down = pre[chip, 4] + pre[chip, 1] * down + pre[chip, 2] * up
+        further = z_stat[n, 1] * down + (z_stat[n, 2] * z_pre[n, 3] + z_push[n, 1])
+        down = jnp.where(zero + (n > z).astype(F32) > 0.5, further, zero)
+        z_pre[n, 4] = down
+    up = z_pre[z, 3]
+    down = z_pre[lax.rem(z + 1, nz), 4]
+    down = jnp.where(zero + (z + 1 < nz).astype(F32) > 0.5, down, zero)
+    for pre, place in ((x_pre, cx), (y_pre, cy)):
+        down = pre[place, 4] + pre[place, 1] * down + pre[place, 2] * up
+        up = pre[place, 3] + pre[place, 0] * up
+    chip_up, chip_down = up, down
     middle = A_0 * chip_up + B_0
     up = jnp.where(first_core, chip_up, middle)
     down = jnp.where(first_core, R_1 * chip_down + C_1 * middle + D_1, chip_down)
@@ -536,18 +681,53 @@
         ends_last, down + s_own * (own_a * up + b_own), own_a * down + s_own * (up + s_own * rhs)
     )
 
-    modes = [jnp.broadcast_to(back[k : k + 1, :], (8, 128)) for k in range(8)]
+    backs[...] = back
+    back_copy = pltpu.make_async_copy(backs, back_out, out_sem.at[2])
+    back_copy.start()
+    spread_z_left(z_stat, 1, stat_send, 1, stat_tail_send)
+    spread_z_left(z_push, 1, push_send, 2, push_tail_send)
+    adv_copy.wait()
+    guess_copy.wait()
+    back_copy.wait()
+
+
+def finish(adv, guess, back, adv_out, prs_out, whole, fg, bk, sem):
+    loads = [
+        pltpu.make_async_copy(back, bk, sem.at[0]),
+        pltpu.make_async_copy(guess, fg, sem.at[1]),
+    ]
+    come, go = [], []
+    for n in range(5):
+        spot = pl.ds(512 * n, 512)
+        come.append(pltpu.make_async_copy(adv.at[spot], whole.at[spot], sem.at[3 + n]))
+        go.append(pltpu.make_async_copy(whole.at[spot], adv_out.at[spot], sem.at[8 + n]))
+    for copy in loads + come:
+        copy.start()
+    row = lax.broadcasted_iota(jnp.int32, (8, 128), 0)
+    gap = []
+    for b in range(2):
+        values = jnp.full((8, 128), float(H[b, 7]), F32)
+        for k in range(7):
+            values = jnp.where(row == k, float(H[b, k]), values)
+        gap.append(values)
+    for copy in loads:
+        copy.wait()
+    modes = [jnp.broadcast_to(bk[k : k + 1, :], (8, 128)) for k in range(8)]
     edges = [gap[0] * modes[2 * k] + gap[1] * modes[2 * k + 1] for k in range(4)]
     for j in range(8):
-        ends = [float(H[0, j]) * edges[2 * a] + float(H[1, j]) * edges[2 * a + 1] for a in range(2)]
+        rims = [float(H[0, j]) * edges[2 * a] + float(H[1, j]) * edges[2 * a + 1] for a in range(2)]
         for i in range(8):
-            spot = tile(fg, 64 * i + 8 * j)
-            spot[...] = spot[...] + float(H[0, i]) * ends[0] + float(H[1, i]) * ends[1]
-    prs_copy = pltpu.make_async_copy(fg, prs_out, out_sem.at[1])
-    prs_copy.start()
-    wait_bytes(slabs.at[0 : nz - 1], slab_sem.at[0])
-    adv_copy.wait()
-    prs_copy.wait()
+            at_ij = 64 * i + 8 * j
+            guessed = fg[at_ij : at_ij + 8, :]
+            fg[at_ij : at_ij + 8, :] = guessed + float(H[0, i]) * rims[0] + float(H[1, i]) * rims[1]
+    out = pltpu.make_async_copy(fg, prs_out, sem.at[2])
+    out.start()
+    for n in range(5):
+        come[n].wait()
+        go[n].start()
+    for copy in go:
+        copy.wait()
+    out.wait()
 
 
 def solution(mesh):
@@ -559,12 +739,15 @@
     anywhere = pl.BlockSpec(memory_space=pl.ANY)
 
     def local(fields, metric, diffusivity, joule_heat, face_flip, coarse_decay):
-        advanced, pressure = pl.pallas_call(
+        fields_shape = jax.ShapeDtypeStruct((2560, 128), F32)
+        node_shape = jax.ShapeDtypeStruct((512, 128), F32)
+        mode_shape = jax.ShapeDtypeStruct((8, 128), F32)
+        advanced, guess, back = pl.pallas_call(
             functools.partial(kernel, (nz, nx, ny)),
             name="step",
-            out_shape=(jax.ShapeDtypeStruct((2560, 128), F32), jax.ShapeDtypeStruct((512, 128), F32)),
+            out_shape=(fields_shape, node_shape, mode_shape),
             in_specs=[anywhere] * 6,
-            out_specs=(anywhere, anywhere),
+            out_specs=(anywhere, anywhere, anywhere),
             scratch_shapes=[
                 vmem(2560, 128),
                 vmem(512, 128),
@@ -580,7 +763,6 @@
                 vmem(512, 128),
                 vmem(128, 128),
                 vmem(256, 128),
-                vmem(nz, 2, 8, 128),
                 vmem(320, 128),
                 vmem(320, 128),
                 vmem(320, 128),
@@ -593,21 +775,33 @@
                 vmem(3, 16, 128),
                 vmem(2, 8, 128),
                 vmem(2, 8, 128),
-                vmem(nx * ny, 2, 8, 128),
-                vmem(nx * ny, 3, 8, 128),
-                vmem(nx * ny, 5, 8, 128),
-                vmem(nz, 2, 8, 128),
-                vmem(nz, 3, 8, 128),
-                dma(6), dma(2), dma(4), dma(4), dma(2), dma(2), dma(3), dma(3),
-                dma(2), dma(2), dma(2), dma(2), dma(2),
+                vmem(2, ny + 2, 8, 128),
+                vmem(2, 8, 128),
+                vmem(8, 128),
+                vmem(ny, 3, 8, 128), vmem(ny, 2, 8, 128), vmem(ny, 5, 8, 128),
+                vmem(nx, 3, 8, 128), vmem(nx, 2, 8, 128), vmem(nx, 5, 8, 128),
+                vmem(nz, 3, 8, 128), vmem(nz, 2, 8, 128), vmem(nz, 5, 8, 128),
+                dma(10), dma(3), dma(4), dma(4), dma(2), dma(2), dma(3), dma(3),
+                dma(2), dma(2), dma(2), dma(2), dma(2), dma(3), dma(3), dma(2), dma(2),
+                dma(nz), dma(nz), dma(nz), dma(nz),
+                pltpu.SemaphoreType.REGULAR((2,)),
             ],
             compiler_params=pltpu.CompilerParams(
-                collective_id=0, has_side_effects=True, vmem_limit_bytes=32 * 1024 * 1024
+                collective_id=0, has_side_effects=True, vmem_limit_bytes=60 * 1024 * 1024
             ),
         )(
             fields.reshape(2560, 128), joule_heat.reshape(512, 128), metric, diffusivity,
             face_flip, coarse_decay.reshape(8, 128),
         )
+        advanced, pressure = pl.pallas_call(
+            finish,
+            name="finish",
+            out_shape=(fields_shape, node_shape),
+            in_specs=[anywhere] * 3,
+            out_specs=(anywhere, anywhere),
+            scratch_shapes=[vmem(2560, 128), vmem(512, 128), vmem(8, 128), dma(13)],
+            compiler_params=pltpu.CompilerParams(vmem_limit_bytes=60 * 1024 * 1024),
+        )(advanced, guess, back)
         return advanced.reshape(5, 512, 1, 128), pressure.reshape(512, 1, 128)
 
     in_specs = (

time: 56.2 us -> 45.2 us (0.80)
  local copies, waits for them, and re-layouts: 6.04 us -> 0 us
  Pallas kernels: 48.6 us -> 43.7 us
    pallas_call x1, Pallas kernels: 48.6 us -> 41.4 us  [local(): pl.pallas_call(functools.partial(kernel, (nz, nx, ny)), name='step', out_...]
    unnamed x12 -> x0, local copies, waits for them, and re-layouts: 6.04 us -> none
    pallas_call x0 -> x1, Pallas kernels: none -> 2.25 us  [local(): pl.pallas_call(finish, name='finish', out_shape=(fields_shape, node_shape...]
where the time goes in v2:
time: 45.2 us; the launch traced here: 45 us
  Pallas kernels  43.7 us (97%)
  between operations  1.29 us (3%)
    pallas_call x1, Pallas kernels, local(): pl.pallas_call(functools.partial(kernel, (nz, nx, ny)), name='step', out_...  41.4 us
    pallas_call x1, Pallas kernels, local(): pl.pallas_call(finish, name='finish', out_shape=(fields_shape, node_shape...  2.25 us

profile of v2, /device:TPU:1, one launch (start us, length us, event | category | flops | bytes accessed | tf_op | source)
XLA Modules:
  0.0 45.0 jit_solution(9277887803853077904)
XLA Ops:
  1.3 41.4 %step.1 = (f32[2560,128]{1,0:T(8,128)}, f32[512,128]{1,0:T(8,128)}, f32[8,128]{1,0:T(8,128)}) custom-call(f32[2560,128]{1,0:T(8,128)} %bitcast.9, f32[512,128]{1,0:T(8,128)} %bitcast.10, f32[3,1,128]{2,1,0:T(1,128)} %metric.1, f32[5]{0:T(128)} %diffusivity.1, s32[1]{0:T(128)S(6)} %copy.10.flip, f32[8,128]{1,0:T(8,128)} %bitcast.11), custom_call_target="tpu_custom_call" | custom-call | tf_op jit(solution)/shard_map/step/pallas_call | solution.py:745
  42.7 2.2 %finish.1 = (f32[2560,128]{1,0:T(8,128)}, f32[512,128]{1,0:T(8,128)}) custom-call(f32[2560,128]{1,0:T(8,128)} %get-tuple-element.7.adv, f32[512,128]{1,0:T(8,128)} %get-tuple-element.8.guess, f32[8,128]{1,0:T(8,128)} %get-tuple-element.9.back), custom_call_target="tpu_custom_call" | custom-call | tf_op jit(solution)/shard_map/finish/pallas_call | solution.py:796

commit v3 on v2

--- a/solution.py
+++ b/solution.py
@@ -9,6 +9,7 @@
 from jax.sharding import PartitionSpec as P
 
 MESH = pl.DeviceIdType.MESH
+CHUNKS = 5
 F32 = jnp.float32
 
 POINTS = np.cos(np.pi * np.arange(8) / 7.0)
@@ -69,10 +70,10 @@
     f, q, met, dif, flp, dec, s, u, tt, dv, fg, res, wgt, proj,
     face_l, face_r, got_l, got_r, pface_l, pface_r, pgot_l, pgot_r,
     near_out, near, mine, partner, rates, edge, backs,
-    y_stat, y_push, y_pre, x_stat, x_push, x_pre, z_stat, z_push, z_pre,
+    y_stat, y_push, y_pre, x_stat, x_push, x_pre, z_all, z_back, z_push, z_pre,
     load_sem, out_sem, face_send, face_recv, pface_send, pface_recv, near_send, near_recv,
     pair_sem, rate_sem, swap_sem, edge_send, edge_recv, push_send, push_recv, stat_send, stat_recv,
-    stat_tail_send, stat_tail_recv, push_tail_send, push_tail_recv, heard,
+    stat_tail_send, stat_tail_recv, push_tail_send, push_tail_recv, both_sem, heard,
 ):
     nz, nx, ny = sizes
     chips_n = nx * ny
@@ -141,35 +142,40 @@
     def wait_bytes(ref, sem):
         pltpu.make_async_copy(ref, ref, sem).wait()
 
+    def offsets(n, wanted):
+        return sorted({d % n for d in wanted} - {0})
+
+    near_x = offsets(nx, (1, 2, 3))
+    near_y = offsets(ny, (1, 2, -1, -2))
+    near_z = offsets(nz, (1, 2, -1, -2))
+    z_back[...] = jnp.zeros((nz, 2, 8, 128), F32)
+    barrier = pltpu.get_barrier_semaphore()
+    targets = [other_core] + [shift(d, 0, 0) for d in near_x]
+    targets += [shift(0, d, 0) for d in near_y] + [shift(0, 0, d) for d in near_z]
+    for condition, device in ((has_outer, outer), (has_inner, inner_two)):
+
+        @pl.when(condition)
+        def _():
+            pl.semaphore_signal(barrier, inc=1, device_id=device, device_id_type=MESH)
+
+    for device in targets:
+        pl.semaphore_signal(barrier, inc=1, device_id=device, device_id_type=MESH)
+    def load(src, dst, rows, k):
+        return pltpu.make_async_copy(src.at[rows], dst.at[rows], load_sem.at[k])
+
     loads = [
         pltpu.make_async_copy(decay, dec, load_sem.at[0]),
         pltpu.make_async_copy(metric, met, load_sem.at[1]),
         pltpu.make_async_copy(flip, flp, load_sem.at[2]),
         pltpu.make_async_copy(diffusivity, dif, load_sem.at[3]),
-        pltpu.make_async_copy(heat, q, load_sem.at[4]),
     ]
-    for n in range(5):
-        spot = pl.ds(512 * n, 512)
-        loads.append(pltpu.make_async_copy(fields.at[spot], f.at[spot], load_sem.at[5 + n]))
-    for copy in loads:
+    loads += [load(fields, f, pl.ds(512 * n, 512), 4 + n) for n in range(3)]
+    ends_of = [512 * n + at_plane for n in (3, 4) for at_plane in (0, 448)]
+    loads += [load(fields, f, pl.ds(spot, 64), 7 + k) for k, spot in enumerate(ends_of)]
+    later = [load(fields, f, pl.ds(512 * n + 64, 384), 8 + n) for n in (3, 4)]
+    later.append(pltpu.make_async_copy(heat, q, load_sem.at[13]))
+    for copy in loads + later:
         copy.start()
-
-    def offsets(n, wanted):
-        return sorted({d % n for d in wanted} - {0})
-
-    near_x = offsets(nx, (1, 2, 3))
-    near_y = offsets(ny, (1, 2, -1, -2))
-    near_z = offsets(nz, (1, 2, -1, -2))
-    barrier = pltpu.get_barrier_semaphore()
-    targets = [other_core] + [shift(d, 0, 0) for d in near_x]
-    targets += [shift(0, d, 0) for d in near_y] + [shift(0, 0, d) for d in near_z]
-    for device in targets:
-        pl.semaphore_signal(barrier, inc=1, device_id=device, device_id_type=MESH)
-    for condition, device in ((has_outer, outer), (has_inner, inner_two)):
-
-        @pl.when(condition)
-        def _():
-            pl.semaphore_signal(barrier, inc=1, device_id=device, device_id_type=MESH)
 
     second = [shift(0, d, 0) for d in offsets(ny, (2, -2))] + [shift(0, 0, d) for d in offsets(nz, (2, -2))]
     third = [shift(0, 0, d) for d in offsets(nz, (4, -4))]
@@ -208,40 +214,51 @@
     def strided(ref, base, k):
         return ref[pl.ds(base + k, 8, stride=8), :]
 
-    def start_plane(i):
+    def start_velocity(i):
         def line(j, carry):
             at_row = i * 64 + j * 8
             x = [tile(f, n * 512 + at_row)[...] for n in range(5)]
-            warm = jnp.tanh(x[3])
-            bubbles = jnp.tanh(0.5 * x[4])
-            heating = tile(q, at_row)[...] * (0.05 + 0.025 * warm) * (0.5 - 0.5 * bubbles)
-            lifting = 0.015 * x[3] - 0.0125 - 0.0125 * bubbles
-            added = [x[0], x[1] + lifting, x[2], x[3] + heating, x[4] + 0.2 * heating]
-            for n in range(5):
-                tile(s, n * 512 + at_row)[...] = added[n]
+            lifting = 0.015 * x[3] - 0.0125 - 0.0125 * jnp.tanh(0.5 * x[4])
             for n in range(3):
+                tile(s, n * 512 + at_row)[...] = x[n] + lifting if n == 1 else x[n]
                 tile(u, n * 512 + at_row)[...] = 0.01 * m[n] * x[n]
             return carry
 
-        lax.fori_loop(0, 8, line, 0, unroll=2)
-
-    def step_plane(n, i):
-        at_row = i * 64
-        base = n * 512 + at_row
+        lax.fori_loop(0, 8, line, 0, unroll=4)
+
+    def start_scalars(i):
+        def line(j, carry):
+            at_row = i * 64 + j * 8
+            warmth, bubbles = tile(f, 1536 + at_row)[...], tile(f, 2048 + at_row)[...]
+            warm, share = 0.05 + 0.025 * jnp.tanh(warmth), 0.5 - 0.5 * jnp.tanh(0.5 * bubbles)
+            heating = tile(q, at_row)[...] * warm * share
+            tile(s, 1536 + at_row)[...] = warmth + heating
+            tile(s, 2048 + at_row)[...] = bubbles + 0.2 * heating
+            return carry
+
+        lax.fori_loop(0, 8, line, 0, unroll=4)
+
+    def step_planes(n, planes):
         rate = dif[n]
         c1, c2 = rate * msq[1], rate * msq[2]
-        even, odd = split([strided(f, base, k) for k in range(8)])
-        for p in range(4):
-            slopes, bends = apply_d(even, odd, p), apply_k(even, odd, p)
-            for k, slope, bend in zip((p, 7 - p), slopes, bends):
-                tt[8 * k : 8 * k + 8, :] = strided(u, 1024 + at_row, k) * slope + c2 * bend
-        even, odd = split([tile(f, base + 8 * j)[...] for j in range(8)])
-        for p in range(4):
-            slopes, bends = apply_d(even, odd, p), apply_k(even, odd, p)
-            for j, slope, bend in zip((p, 7 - p), slopes, bends):
-                gone = tile(u, 512 + at_row + 8 * j)[...] * slope + c1 * bend
-                gone = gone + strided(tt, 0, j)
-                tile(s, base + 8 * j)[...] = tile(s, base + 8 * j)[...] - gone
+        for slot, i in enumerate(planes):
+            at_row = i * 64
+            even, odd = split([strided(f, n * 512 + at_row, k) for k in range(8)])
+            for p in range(4):
+                slopes, bends = apply_d(even, odd, p), apply_k(even, odd, p)
+                for k, slope, bend in zip((p, 7 - p), slopes, bends):
+                    spot = 64 * slot + 8 * k
+                    tt[spot : spot + 8, :] = strided(u, 1024 + at_row, k) * slope + c2 * bend
+        for slot, i in enumerate(planes):
+            at_row = i * 64
+            base = n * 512 + at_row
+            even, odd = split([tile(f, base + 8 * j)[...] for j in range(8)])
+            for p in range(4):
+                slopes, bends = apply_d(even, odd, p), apply_k(even, odd, p)
+                for j, slope, bend in zip((p, 7 - p), slopes, bends):
+                    gone = tile(u, 512 + at_row + 8 * j)[...] * slope + c1 * bend
+                    gone = gone + strided(tt, 64 * slot, j)
+                    tile(s, base + 8 * j)[...] = tile(s, base + 8 * j)[...] - gone
 
     def step_lines(n, pairs):
         c0 = dif[n] * msq[0]
@@ -257,7 +274,7 @@
                     tile(s, base + 64 * i)[...] = keep * (tile(s, base + 64 * i)[...] - gone)
             return carry
 
-        lax.fori_loop(0, 8, line, 0, unroll=2)
+        lax.fori_loop(0, 8, line, 0, unroll=4)
 
     def join_span(ref, base):
         low, high = tile(ref, base), tile(ref, base + 56)
@@ -271,22 +288,21 @@
             tile(face_l, spot)[...] = oriented(tile(s, n * 512 + 8 * j)[...])
             tile(face_r, spot)[...] = tile(s, n * 512 + 448 + 8 * j)[...]
 
-    def each(low, high, body):
+    def each(low, high, body, unroll=1):
         def run(n, carry):
             body(n)
             return carry
 
-        lax.fori_loop(low, high, run, 0)
+        lax.fori_loop(low, high, run, 0, unroll=unroll)
 
     near_out[0:8, :] = dec[...]
     near_out[8:16, :] = zero + flp[0].astype(F32)
 
     for i in (0, 7):
-        start_plane(i)
+        start_velocity(i)
 
     def velocity_faces(n):
-        for i in (0, 7):
-            step_plane(n, i)
+        step_planes(n, (0, 7))
         step_lines(n, (0,))
         for i in (0, 7):
             join_span(s, n * 512 + i * 64)
@@ -295,6 +311,19 @@
     each(0, 2, velocity_faces)
 
     pl.semaphore_wait(barrier, len(targets) + 2 * has_outer.astype(jnp.int32))
+    def chain_exchange(left, right, from_left, from_right, sems, k):
+        ahead, behind = jnp.logical_not(at_end), jnp.logical_not(at_start)
+        return Exchange([
+            (behind, ahead, (left, from_right, sems[0].at[k], sems[1].at[k], before)),
+            (ahead, behind, (right, from_left, sems[0].at[k + 1], sems[1].at[k + 1], after)),
+        ])
+
+    def face_exchange(n, count, k):
+        rows = pl.ds(n * 64, count * 64)
+        return chain_exchange(
+            face_l.at[rows], face_r.at[rows], got_l.at[rows], got_r.at[rows], (face_send, face_recv), k
+        )
+
     pass_word(0, second)
     nears = Exchange([
         (None, None, (near_out, near.at[0], near_send.at[0], near_recv.at[0], other_core)),
@@ -308,31 +337,22 @@
         def _():
             near[k] = jnp.zeros((16, 128), F32)
 
+    for n in range(2):
+        face_exchange(n, 1, 2 * n).start()
     each(2, 3, velocity_faces)
 
-    def chain_exchange(left, right, from_left, from_right, sems, k):
-        ahead, behind = jnp.logical_not(at_end), jnp.logical_not(at_start)
-        return Exchange([
-            (behind, ahead, (left, from_right, sems[0].at[k], sems[1].at[k], before)),
-            (ahead, behind, (right, from_left, sems[0].at[k + 1], sems[1].at[k + 1], after)),
-        ])
-
-    part = slice(0, 192)
-    velocity_exchange = chain_exchange(
-        face_l.at[part], face_r.at[part], got_l.at[part], got_r.at[part], (face_send, face_recv), 0
-    )
-    velocity_exchange.start()
-
-    for p in (1, 2, 3):
-        for i in (p, 7 - p):
-            start_plane(i)
+    face_exchange(2, 1, 4).start()
+
+    for copy in later:
+        copy.wait()
+    each(1, 7, start_velocity)
 
     def velocity_rest(n):
-        def plane(i, carry):
-            step_plane(n, i)
+        def planes(t, carry):
+            step_planes(n, (1 + 2 * t, 2 + 2 * t))
             return carry
 
-        lax.fori_loop(1, 7, plane, 0)
+        lax.fori_loop(0, 3, planes, 0)
         step_lines(n, (1, 2, 3))
         for i in range(1, 7):
             join_span(s, n * 512 + i * 64)
@@ -392,7 +412,8 @@
     k_4 = jnp.where(ends_last, a_before * s_own * k_2 + s_before * s_before, 0.0)
     flip_after = jnp.where(first_core, near[0, 8:16, :], near[1, 8:16, :]) == 1.0
 
-    velocity_exchange.wait()
+    for n in range(3):
+        face_exchange(n, 1, 2 * n).wait()
     start_mask, end_mask = zero + not_start > 0.5, zero + not_end > 0.5
 
     def join_chain(n):
@@ -404,18 +425,22 @@
 
     each(0, 3, join_chain)
 
-    def divergence_plane(i):
-        at_row = i * 64
-        even, odd = split([strided(s, 1024 + at_row, k) for k in range(8)])
-        for p in range(4):
-            for k, slope in zip((p, 7 - p), apply_d(even, odd, p)):
-                tt[8 * k : 8 * k + 8, :] = m[2] * slope
-        even, odd = split([tile(s, 512 + at_row + 8 * j)[...] for j in range(8)])
-        for p in range(4):
-            for j, slope in zip((p, 7 - p), apply_d(even, odd, p)):
-                tile(dv, at_row + 8 * j)[...] = m[1] * slope + strided(tt, 0, j)
-
-    each(0, 8, divergence_plane)
+    def divergence_planes(t):
+        for slot in range(2):
+            at_row = (2 * t + slot) * 64
+            even, odd = split([strided(s, 1024 + at_row, k) for k in range(8)])
+            for p in range(4):
+                for k, slope in zip((p, 7 - p), apply_d(even, odd, p)):
+                    spot = 64 * slot + 8 * k
+                    tt[spot : spot + 8, :] = m[2] * slope
+        for slot in range(2):
+            at_row = (2 * t + slot) * 64
+            even, odd = split([tile(s, 512 + at_row + 8 * j)[...] for j in range(8)])
+            for p in range(4):
+                for j, slope in zip((p, 7 - p), apply_d(even, odd, p)):
+                    tile(dv, at_row + 8 * j)[...] = m[1] * slope + strided(tt, 64 * slot, j)
+
+    each(0, 4, divergence_planes)
 
     def guess_line(j):
         even, odd = split([tile(s, 64 * i + 8 * j)[...] for i in range(8)])
@@ -428,22 +453,26 @@
                 spot[...] = whole
                 tile(fg, 64 * i + 8 * j)[...] = weight * whole
 
-    each(0, 8, guess_line)
-
-    def residual_plane(i):
-        at_row = i * 64
-        even, odd = split([strided(fg, at_row, k) for k in range(8)])
-        for p in range(4):
-            for k, bend in zip((p, 7 - p), apply_k(even, odd, p)):
-                tt[8 * k : 8 * k + 8, :] = msq[2] * bend
-        even, odd = split([tile(fg, at_row + 8 * j)[...] for j in range(8)])
-        for p in range(4):
-            for j, bend in zip((p, 7 - p), apply_k(even, odd, p)):
-                at_j = at_row + 8 * j
-                gone = tile(fg, at_j)[...] + msq[1] * bend + strided(tt, 0, j)
-                tile(res, at_j)[...] = tile(dv, at_j)[...] - gone
-
-    each(0, 8, residual_plane)
+    each(0, 8, guess_line, 2)
+
+    def residual_planes(t):
+        for slot in range(2):
+            at_row = (2 * t + slot) * 64
+            even, odd = split([strided(fg, at_row, k) for k in range(8)])
+            for p in range(4):
+                for k, bend in zip((p, 7 - p), apply_k(even, odd, p)):
+                    spot = 64 * slot + 8 * k
+                    tt[spot : spot + 8, :] = msq[2] * bend
+        for slot in range(2):
+            at_row = (2 * t + slot) * 64
+            even, odd = split([tile(fg, at_row + 8 * j)[...] for j in range(8)])
+            for p in range(4):
+                for j, bend in zip((p, 7 - p), apply_k(even, odd, p)):
+                    at_j = at_row + 8 * j
+                    gone = tile(fg, at_j)[...] + msq[1] * bend + strided(tt, 64 * slot, j)
+                    tile(res, at_j)[...] = tile(dv, at_j)[...] - gone
+
+    each(0, 4, residual_planes)
 
     def project_line(j):
         even, odd = split([tile(fg, 64 * i + 8 * j)[...] for i in range(8)])
@@ -458,7 +487,7 @@
         for n, part in enumerate((low, high, left[7], left[0])):
             tile(proj, n * 64 + 8 * j)[...] = part
 
-    each(0, 8, project_line)
+    each(0, 8, project_line, 4)
 
     gap = [by_row(H[0]), by_row(H[1])]
     sums = []
@@ -539,7 +568,7 @@
             def _():
                 wait_bytes(ref.at[z, rest], tail_sem.at[d])
 
-    z_stat_tail, z_push_tail = (stat_tail_send, stat_tail_recv), (push_tail_send, push_tail_recv)
+    z_push_tail = (push_tail_send, push_tail_recv)
     spread(y_push, cy, 0, pushes, y_peers)
 
     wait_bytes(rates.at[core, pl.ds(1, ny - 1)], rate_sem.at[1])
@@ -596,12 +625,14 @@
     set_stat(x_stat, cx, combine_stat(y_stat, y_pre, ny))
     spread(x_stat, cx, 0, stats, x_peers)
 
+    each(0, 8, start_scalars)
+
     def scalars(n):
-        def plane(i, carry):
-            step_plane(n, i)
+        def planes(t, carry):
+            step_planes(n, (2 * t, 2 * t + 1))
             return carry
 
-        lax.fori_loop(0, 8, plane, 0)
+        lax.fori_loop(0, 4, planes, 0)
         step_lines(n, (0, 1, 2, 3))
         for i in range(8):
             join_span(s, n * 512 + i * 64)
@@ -614,21 +645,34 @@
         tile(pface_l, 8 * j)[...] = oriented(tile(fg, 8 * j)[...])
         tile(pface_r, 8 * j)[...] = tile(fg, 448 + 8 * j)[...]
 
-    pl.semaphore_wait(heard.at[1], len(third)) if third else None
-    spread_ended(x_stat, 0, stat_recv, x_peers)
-    set_stat(z_stat, z, combine_stat(x_stat, x_pre, nx))
-    spread_z(z_stat, 1, stats, 1, z_stat_tail)
-
     spread_ended(y_push, 0, push_recv, y_peers)
     set_stat(x_push, cx, combine_push(y_stat, y_push, y_pre, ny))
     spread(x_push, cx, 1, pushes, x_peers)
+    pl.semaphore_wait(heard.at[1], len(third)) if third else None
+    spread_ended(x_stat, 0, stat_recv, x_peers)
+    slab_a, slab_r, slab_c = combine_stat(x_stat, x_pre, nx)
+
+    @pl.when(core == 0)
+    def _():
+        z_all[z] = slab_a
+        for device in z_peers:
+            send(z_all.at[z], z_all.at[z], stat_send.at[1], stat_recv.at[1], device)
+
+    @pl.when(core == 1)
+    def _():
+        z_back[z, 0] = slab_r
+        z_back[z, 1] = slab_c
+
+    for d, device in zip(z_order, z_peers):
+
+        @pl.when((core == 1) & (z + d >= nz))
+        def _():
+            send(z_back.at[z], z_back.at[z], stat_tail_send.at[d], stat_tail_recv.at[z], device)
+
+
     guess_exchange = chain_exchange(pface_l, pface_r, pgot_l, pgot_r, (pface_send, pface_recv), 0)
     guess_exchange.start()
-    part = slice(192, 320)
-    scalar_exchange = chain_exchange(
-        face_l.at[part], face_r.at[part], got_l.at[part], got_r.at[part], (face_send, face_recv), 2
-    )
-    scalar_exchange.start()
+    face_exchange(3, 2, 6).start()
     spread_ended(x_push, 1, push_recv, x_peers)
     set_stat(z_push, z, combine_push(x_stat, x_push, x_pre, nx))
     spread_z(z_push, 1, pushes, 2, z_push_tail)
@@ -647,7 +691,7 @@
         low, high = tile(fg, 8 * j), tile(fg, 448 + 8 * j)
         low[...] = jnp.where(start_mask, 0.5 * (low[...] + oriented(tile(pgot_l, 8 * j)[...])), low[...])
         high[...] = jnp.where(end_mask, 0.5 * (high[...] + tile(pgot_r, 8 * j)[...]), high[...])
-    scalar_exchange.wait()
+    face_exchange(3, 2, 6).wait()
     each(3, 5, join_chain)
     adv_copy = pltpu.make_async_copy(s, adv_out, out_sem.at[0])
     adv_copy.start()
@@ -655,16 +699,36 @@
     guess_copy = pltpu.make_async_copy(fg, guess_out, out_sem.at[1])
     guess_copy.start()
 
-    spread_z_got(z_stat, 1, stat_recv, 1, stat_tail_recv)
+    all_share = remote(z_all, z_all, both_sem.at[0], both_sem.at[1], other_core)
+    back_share = remote(z_back, z_back, both_sem.at[2], both_sem.at[3], other_core)
+    for n in range(1, nz):
+
+        @pl.when((core == 1) & (z < n))
+        def _():
+            wait_bytes(z_back.at[n], stat_tail_recv.at[n])
+
+    @pl.when(core == 1)
+    def _():
+        back_share.start()
+        all_share.wait_recv()
+        back_share.wait_send()
+
+    @pl.when(core == 0)
+    def _():
+        wait_bytes(z_all.at[0 : nz - 1], stat_recv.at[1])
+        all_share.start()
+        back_share.wait_recv()
+        all_share.wait_send()
+
     spread_z_got(z_push, 1, push_recv, 2, push_tail_recv)
 
     up = zero
     for n in range(nz):
         z_pre[n, 3] = up
-        up = z_stat[n, 0] * up + z_push[n, 0]
+        up = z_all[n] * up + z_push[n, 0]
     down = zero
     for n in range(nz - 1, -1, -1):
-        further = z_stat[n, 1] * down + (z_stat[n, 2] * z_pre[n, 3] + z_push[n, 1])
+        further = z_back[n, 0] * down + (z_back[n, 1] * z_pre[n, 3] + z_push[n, 1])
         down = jnp.where(zero + (n > z).astype(F32) > 0.5, further, zero)
         z_pre[n, 4] = down
     up = z_pre[z, 3]
@@ -684,7 +748,17 @@
     backs[...] = back
     back_copy = pltpu.make_async_copy(backs, back_out, out_sem.at[2])
     back_copy.start()
-    spread_z_left(z_stat, 1, stat_send, 1, stat_tail_send)
+
+    @pl.when(core == 0)
+    def _():
+        wait_bytes(z_all.at[0 : nz - 1], stat_send.at[1])
+
+    for d in range(1, nz):
+
+        @pl.when((core == 1) & (z + d >= nz))
+        def _():
+            wait_bytes(z_back.at[z], stat_tail_send.at[d])
+
     spread_z_left(z_push, 1, push_send, 2, push_tail_send)
     adv_copy.wait()
     guess_copy.wait()
@@ -697,10 +771,10 @@
         pltpu.make_async_copy(guess, fg, sem.at[1]),
     ]
     come, go = [], []
-    for n in range(5):
-        spot = pl.ds(512 * n, 512)
+    for n in range(CHUNKS):
+        spot = pl.ds(n * (2560 // CHUNKS), 2560 // CHUNKS)
         come.append(pltpu.make_async_copy(adv.at[spot], whole.at[spot], sem.at[3 + n]))
-        go.append(pltpu.make_async_copy(whole.at[spot], adv_out.at[spot], sem.at[8 + n]))
+        go.append(pltpu.make_async_copy(whole.at[spot], adv_out.at[spot], sem.at[3 + CHUNKS + n]))
     for copy in loads + come:
         copy.start()
     row = lax.broadcasted_iota(jnp.int32, (8, 128), 0)
@@ -722,7 +796,7 @@
             fg[at_ij : at_ij + 8, :] = guessed + float(H[0, i]) * rims[0] + float(H[1, i]) * rims[1]
     out = pltpu.make_async_copy(fg, prs_out, sem.at[2])
     out.start()
-    for n in range(5):
+    for n in range(CHUNKS):
         come[n].wait()
         go[n].start()
     for copy in go:
@@ -757,7 +831,7 @@
                 vmem(8, 128),
                 vmem(2560, 128),
                 vmem(1536, 128),
-                vmem(64, 128),
+                vmem(128, 128),
                 vmem(512, 128),
                 vmem(512, 128),
                 vmem(512, 128),
@@ -780,10 +854,10 @@
                 vmem(8, 128),
                 vmem(ny, 3, 8, 128), vmem(ny, 2, 8, 128), vmem(ny, 5, 8, 128),
                 vmem(nx, 3, 8, 128), vmem(nx, 2, 8, 128), vmem(nx, 5, 8, 128),
-                vmem(nz, 3, 8, 128), vmem(nz, 2, 8, 128), vmem(nz, 5, 8, 128),
-                dma(10), dma(3), dma(4), dma(4), dma(2), dma(2), dma(3), dma(3),
+                vmem(nz, 8, 128), vmem(nz, 2, 8, 128), vmem(nz, 2, 8, 128), vmem(nz, 5, 8, 128),
+                dma(14), dma(3), dma(8), dma(8), dma(2), dma(2), dma(3), dma(3),
                 dma(2), dma(2), dma(2), dma(2), dma(2), dma(3), dma(3), dma(2), dma(2),
-                dma(nz), dma(nz), dma(nz), dma(nz),
+                dma(nz), dma(nz), dma(nz), dma(nz), dma(4),
                 pltpu.SemaphoreType.REGULAR((2,)),
             ],
             compiler_params=pltpu.CompilerParams(
@@ -799,7 +873,7 @@
             out_shape=(fields_shape, node_shape),
             in_specs=[anywhere] * 3,
             out_specs=(anywhere, anywhere),
-            scratch_shapes=[vmem(2560, 128), vmem(512, 128), vmem(8, 128), dma(13)],
+            scratch_shapes=[vmem(2560, 128), vmem(512, 128), vmem(8, 128), dma(3 + 2 * CHUNKS)],
             compiler_params=pltpu.CompilerParams(vmem_limit_bytes=60 * 1024 * 1024),
         )(advanced, guess, back)
         return advanced.reshape(5, 512, 1, 128), pressure.reshape(512, 1, 128)

time: 45.2 us -> 43.1 us (0.954)
  Pallas kernels: 43.7 us -> 41.5 us
    pallas_call x1, Pallas kernels: 41.4 us -> 39.3 us  [local(): pl.pallas_call(functools.partial(kernel, (nz, nx, ny)), name='step', out_...]
where the time goes in v3:
time: 43.1 us; the launch traced here: 42.8 us
  Pallas kernels  41.5 us (96%)
  between operations  1.29 us (3%)
    pallas_call x1, Pallas kernels, local(): pl.pallas_call(functools.partial(kernel, (nz, nx, ny)), name='step', out_...  39.3 us
    pallas_call x1, Pallas kernels, local(): pl.pallas_call(finish, name='finish', out_shape=(fields_shape, node_shape...  2.25 us

profile of v3, /device:TPU:1, one launch (start us, length us, event | category | flops | bytes accessed | tf_op | source)
XLA Modules:
  0.0 42.8 jit_solution(12988317818921576628)
XLA Ops:
  1.3 39.3 %step.1 = (f32[2560,128]{1,0:T(8,128)}, f32[512,128]{1,0:T(8,128)}, f32[8,128]{1,0:T(8,128)}) custom-call(f32[2560,128]{1,0:T(8,128)} %bitcast.9, f32[512,128]{1,0:T(8,128)} %bitcast.10, f32[3,1,128]{2,1,0:T(1,128)} %metric.1, f32[5]{0:T(128)} %diffusivity.1, s32[1]{0:T(128)S(6)} %copy.10.flip, f32[8,128]{1,0:T(8,128)} %bitcast.11), custom_call_target="tpu_custom_call" | custom-call | tf_op jit(solution)/shard_map/step/pallas_call | solution.py:819
  40.6 2.2 %finish.1 = (f32[2560,128]{1,0:T(8,128)}, f32[512,128]{1,0:T(8,128)}) custom-call(f32[2560,128]{1,0:T(8,128)} %get-tuple-element.7.adv, f32[512,128]{1,0:T(8,128)} %get-tuple-element.8.guess, f32[8,128]{1,0:T(8,128)} %get-tuple-element.9.back), custom_call_target="tpu_custom_call" | custom-call | tf_op jit(solution)/shard_map/finish/pallas_call | solution.py:870

commit v4 on v3

--- a/solution.py
+++ b/solution.py
@@ -9,7 +9,6 @@
 from jax.sharding import PartitionSpec as P
 
 MESH = pl.DeviceIdType.MESH
-CHUNKS = 5
 F32 = jnp.float32
 
 POINTS = np.cos(np.pi * np.arange(8) / 7.0)
@@ -66,12 +65,12 @@
 
 
 def kernel(
-    sizes, fields, heat, metric, diffusivity, flip, decay, adv_out, guess_out, back_out,
-    f, q, met, dif, flp, dec, s, u, tt, dv, fg, res, wgt, proj,
+    sizes, fields, heat, metric, diffusivity, flip, decay, s, fg, backs,
+    f, q, met, dif, flp, dec, u, tt, dv, res, wgt, proj,
     face_l, face_r, got_l, got_r, pface_l, pface_r, pgot_l, pgot_r,
-    near_out, near, mine, partner, rates, edge, backs,
+    near_out, near, mine, partner, rates, edge,
     y_stat, y_push, y_pre, x_stat, x_push, x_pre, z_all, z_back, z_push, z_pre,
-    load_sem, out_sem, face_send, face_recv, pface_send, pface_recv, near_send, near_recv,
+    load_sem, face_send, face_recv, pface_send, pface_recv, near_send, near_recv,
     pair_sem, rate_sem, swap_sem, edge_send, edge_recv, push_send, push_recv, stat_send, stat_recv,
     stat_tail_send, stat_tail_recv, push_tail_send, push_tail_recv, both_sem, heard,
 ):
@@ -174,7 +173,7 @@
     loads += [load(fields, f, pl.ds(spot, 64), 7 + k) for k, spot in enumerate(ends_of)]
     later = [load(fields, f, pl.ds(512 * n + 64, 384), 8 + n) for n in (3, 4)]
     later.append(pltpu.make_async_copy(heat, q, load_sem.at[13]))
-    for copy in loads + later:
+    for copy in loads:
         copy.start()
 
     second = [shift(0, d, 0) for d in offsets(ny, (2, -2))] + [shift(0, 0, d) for d in offsets(nz, (2, -2))]
@@ -186,6 +185,8 @@
 
     for copy in loads:
         copy.wait()
+    for copy in later:
+        copy.start()
 
     row = lax.broadcasted_iota(jnp.int32, (8, 128), 0)
     zero = jnp.zeros((8, 128), F32)
@@ -308,7 +309,7 @@
             join_span(s, n * 512 + i * 64)
         stage_faces(n)
 
-    each(0, 2, velocity_faces)
+    each(0, 3, velocity_faces)
 
     pl.semaphore_wait(barrier, len(targets) + 2 * has_outer.astype(jnp.int32))
     def chain_exchange(left, right, from_left, from_right, sems, k):
@@ -337,11 +338,8 @@
         def _():
             near[k] = jnp.zeros((16, 128), F32)
 
-    for n in range(2):
+    for n in range(3):
         face_exchange(n, 1, 2 * n).start()
-    each(2, 3, velocity_faces)
-
-    face_exchange(2, 1, 4).start()
 
     for copy in later:
         copy.wait()
@@ -440,7 +438,7 @@
                 for j, slope in zip((p, 7 - p), apply_d(even, odd, p)):
                     tile(dv, at_row + 8 * j)[...] = m[1] * slope + strided(tt, 64 * slot, j)
 
-    each(0, 4, divergence_planes)
+    each(0, 4, divergence_planes, 2)
 
     def guess_line(j):
         even, odd = split([tile(s, 64 * i + 8 * j)[...] for i in range(8)])
@@ -453,7 +451,7 @@
                 spot[...] = whole
                 tile(fg, 64 * i + 8 * j)[...] = weight * whole
 
-    each(0, 8, guess_line, 2)
+    each(0, 8, guess_line, 4)
 
     def residual_planes(t):
         for slot in range(2):
@@ -472,7 +470,7 @@
                     gone = tile(fg, at_j)[...] + msq[1] * bend + strided(tt, 64 * slot, j)
                     tile(res, at_j)[...] = tile(dv, at_j)[...] - gone
 
-    each(0, 4, residual_planes)
+    each(0, 4, residual_planes, 2)
 
     def project_line(j):
         even, odd = split([tile(fg, 64 * i + 8 * j)[...] for i in range(8)])
@@ -487,7 +485,7 @@
         for n, part in enumerate((low, high, left[7], left[0])):
             tile(proj, n * 64 + 8 * j)[...] = part
 
-    each(0, 8, project_line, 4)
+    each(0, 8, project_line, 8)
 
     gap = [by_row(H[0]), by_row(H[1])]
     sums = []
@@ -693,11 +691,7 @@
         high[...] = jnp.where(end_mask, 0.5 * (high[...] + tile(pgot_r, 8 * j)[...]), high[...])
     face_exchange(3, 2, 6).wait()
     each(3, 5, join_chain)
-    adv_copy = pltpu.make_async_copy(s, adv_out, out_sem.at[0])
-    adv_copy.start()
-
-    guess_copy = pltpu.make_async_copy(fg, guess_out, out_sem.at[1])
-    guess_copy.start()
+
 
     all_share = remote(z_all, z_all, both_sem.at[0], both_sem.at[1], other_core)
     back_share = remote(z_back, z_back, both_sem.at[2], both_sem.at[3], other_core)
@@ -746,8 +740,6 @@
     )
 
     backs[...] = back
-    back_copy = pltpu.make_async_copy(backs, back_out, out_sem.at[2])
-    back_copy.start()
 
     @pl.when(core == 0)
     def _():
@@ -760,23 +752,11 @@
             wait_bytes(z_back.at[z], stat_tail_send.at[d])
 
     spread_z_left(z_push, 1, push_send, 2, push_tail_send)
-    adv_copy.wait()
-    guess_copy.wait()
-    back_copy.wait()
-
-
-def finish(adv, guess, back, adv_out, prs_out, whole, fg, bk, sem):
-    loads = [
-        pltpu.make_async_copy(back, bk, sem.at[0]),
-        pltpu.make_async_copy(guess, fg, sem.at[1]),
-    ]
-    come, go = [], []
-    for n in range(CHUNKS):
-        spot = pl.ds(n * (2560 // CHUNKS), 2560 // CHUNKS)
-        come.append(pltpu.make_async_copy(adv.at[spot], whole.at[spot], sem.at[3 + n]))
-        go.append(pltpu.make_async_copy(whole.at[spot], adv_out.at[spot], sem.at[3 + CHUNKS + n]))
-    for copy in loads + come:
-        copy.start()
+
+
+def finish(adv, guess, back, adv_out, prs_out, fg, sem):
+    move = pltpu.make_async_copy(adv, adv_out, sem.at[0])
+    move.start()
     row = lax.broadcasted_iota(jnp.int32, (8, 128), 0)
     gap = []
     for b in range(2):
@@ -784,23 +764,17 @@
         for k in range(7):
             values = jnp.where(row == k, float(H[b, k]), values)
         gap.append(values)
-    for copy in loads:
-        copy.wait()
-    modes = [jnp.broadcast_to(bk[k : k + 1, :], (8, 128)) for k in range(8)]
+    modes = [jnp.broadcast_to(back[k : k + 1, :], (8, 128)) for k in range(8)]
     edges = [gap[0] * modes[2 * k] + gap[1] * modes[2 * k + 1] for k in range(4)]
     for j in range(8):
         rims = [float(H[0, j]) * edges[2 * a] + float(H[1, j]) * edges[2 * a + 1] for a in range(2)]
         for i in range(8):
             at_ij = 64 * i + 8 * j
-            guessed = fg[at_ij : at_ij + 8, :]
+            guessed = guess[at_ij : at_ij + 8, :]
             fg[at_ij : at_ij + 8, :] = guessed + float(H[0, i]) * rims[0] + float(H[1, i]) * rims[1]
-    out = pltpu.make_async_copy(fg, prs_out, sem.at[2])
+    out = pltpu.make_async_copy(fg, prs_out, sem.at[1])
     out.start()
-    for n in range(CHUNKS):
-        come[n].wait()
-        go[n].start()
-    for copy in go:
-        copy.wait()
+    move.wait()
     out.wait()
 
 
@@ -811,6 +785,7 @@
     vmem = lambda *shape: pltpu.VMEM(shape, F32)
     dma = lambda n: pltpu.SemaphoreType.DMA((n,))
     anywhere = pl.BlockSpec(memory_space=pl.ANY)
+    inside = pl.BlockSpec(memory_space=pltpu.VMEM)
 
     def local(fields, metric, diffusivity, joule_heat, face_flip, coarse_decay):
         fields_shape = jax.ShapeDtypeStruct((2560, 128), F32)
@@ -819,9 +794,9 @@
         advanced, guess, back = pl.pallas_call(
             functools.partial(kernel, (nz, nx, ny)),
             name="step",
-            out_shape=(fields_shape, node_shape, mode_shape),
+            out_shape=(pltpu.VMEM((2560, 128), F32), pltpu.VMEM((512, 128), F32), pltpu.VMEM((8, 128), F32)),
             in_specs=[anywhere] * 6,
-            out_specs=(anywhere, anywhere, anywhere),
+            out_specs=(inside, inside, inside),
             scratch_shapes=[
                 vmem(2560, 128),
                 vmem(512, 128),
@@ -829,10 +804,8 @@
                 pltpu.SMEM((5,), F32),
                 pltpu.SMEM((1,), jnp.int32),
                 vmem(8, 128),
-                vmem(2560, 128),
                 vmem(1536, 128),
                 vmem(128, 128),
-                vmem(512, 128),
                 vmem(512, 128),
                 vmem(512, 128),
                 vmem(128, 128),
@@ -851,11 +824,10 @@
                 vmem(2, 8, 128),
                 vmem(2, ny + 2, 8, 128),
                 vmem(2, 8, 128),
-                vmem(8, 128),
                 vmem(ny, 3, 8, 128), vmem(ny, 2, 8, 128), vmem(ny, 5, 8, 128),
                 vmem(nx, 3, 8, 128), vmem(nx, 2, 8, 128), vmem(nx, 5, 8, 128),
                 vmem(nz, 8, 128), vmem(nz, 2, 8, 128), vmem(nz, 2, 8, 128), vmem(nz, 5, 8, 128),
-                dma(14), dma(3), dma(8), dma(8), dma(2), dma(2), dma(3), dma(3),
+                dma(14), dma(8), dma(8), dma(2), dma(2), dma(3), dma(3),
                 dma(2), dma(2), dma(2), dma(2), dma(2), dma(3), dma(3), dma(2), dma(2),
                 dma(nz), dma(nz), dma(nz), dma(nz), dma(4),
                 pltpu.SemaphoreType.REGULAR((2,)),
@@ -871,10 +843,10 @@
             finish,
             name="finish",
             out_shape=(fields_shape, node_shape),
-            in_specs=[anywhere] * 3,
+            in_specs=[inside] * 3,
             out_specs=(anywhere, anywhere),
-            scratch_shapes=[vmem(2560, 128), vmem(512, 128), vmem(8, 128), dma(3 + 2 * CHUNKS)],
-            compiler_params=pltpu.CompilerParams(vmem_limit_bytes=60 * 1024 * 1024),
+            scratch_shapes=[vmem(512, 128), dma(2)],
+            compiler_params=pltpu.CompilerParams(vmem_limit_bytes=16 * 1024 * 1024),
         )(advanced, guess, back)
         return advanced.reshape(5, 512, 1, 128), pressure.reshape(512, 1, 128)
 

time: 43.1 us -> 41.4 us (0.961)
  Pallas kernels: 41.5 us -> 39.8 us
    pallas_call x1, Pallas kernels: 2.25 us -> 1.15 us  [local(): pl.pallas_call(finish, name='finish', out_shape=(fields_shape, node_shape...]
    pallas_call x1, Pallas kernels: 39.3 us -> 38.7 us  [local(): pl.pallas_call(functools.partial(kernel, (nz, nx, ny)), name='step', out_...]
where the time goes in v4:
time: 41.4 us; the launch traced here: 41.1 us
  Pallas kernels  39.8 us (96%)
  between operations  1.29 us (3%)
    pallas_call x1, Pallas kernels, local(): pl.pallas_call(functools.partial(kernel, (nz, nx, ny)), name='step', out_...  38.7 us
    pallas_call x1, Pallas kernels, local(): pl.pallas_call(finish, name='finish', out_shape=(fields_shape, node_shape...  1.15 us

profile of v4, /device:TPU:1, one launch (start us, length us, event | category | flops | bytes accessed | tf_op | source)
XLA Modules:
  0.0 41.1 jit_solution(6207708004774020395)
XLA Ops:
  1.3 38.7 %step.1 = (f32[2560,128]{1,0:T(8,128)S(1)}, f32[512,128]{1,0:T(8,128)S(1)}, f32[8,128]{1,0:T(8,128)S(1)}) custom-call(f32[2560,128]{1,0:T(8,128)} %bitcast.9, f32[512,128]{1,0:T(8,128)} %bitcast.10, f32[3,1,128]{2,1,0:T(1,128)} %metric.1, f32[5]{0:T(128)} %diffusivity.1, s32[1]{0:T(128)S(6)} %copy.10.flip, f32[8,128]{1,0:T(8,128)} %bitcast.11), custom_call_target="tpu_custom_call" | custom-call | tf_op jit(solution)/shard_map/step/pallas_call | solution.py:794
  40.0 1.2 %finish.1 = (f32[2560,128]{1,0:T(8,128)}, f32[512,128]{1,0:T(8,128)}) custom-call(f32[2560,128]{1,0:T(8,128)S(1)} %get-tuple-element.7.adv, f32[512,128]{1,0:T(8,128)S(1)} %get-tuple-element.8.guess, f32[8,128]{1,0:T(8,128)S(1)} %get-tuple-element.9.back), custom_call_target="tpu_custom_call" | custom-call | tf_op jit(solution)/shard_map/finish/pallas_call | solution.py:842

commit v5 on v4

--- a/solution.py
+++ b/solution.py
@@ -684,6 +684,23 @@
         def _():
             wait_bytes(rates.at[0, pl.ds(1, ny - 1)], edge_send.at[k])
 
+    all_share = remote(z_all, z_all, both_sem.at[0], both_sem.at[1], other_core)
+    back_share = remote(z_back, z_back, both_sem.at[2], both_sem.at[3], other_core)
+    for n in range(1, nz):
+
+        @pl.when((core == 1) & (z < n))
+        def _():
+            wait_bytes(z_back.at[n], stat_tail_recv.at[n])
+
+    @pl.when(core == 1)
+    def _():
+        back_share.start()
+
+    @pl.when(core == 0)
+    def _():
+        wait_bytes(z_all.at[0 : nz - 1], stat_recv.at[1])
+        all_share.start()
+
     guess_exchange.wait()
     for j in range(8):
         low, high = tile(fg, 8 * j), tile(fg, 448 + 8 * j)
@@ -693,24 +710,13 @@
     each(3, 5, join_chain)
 
 
-    all_share = remote(z_all, z_all, both_sem.at[0], both_sem.at[1], other_core)
-    back_share = remote(z_back, z_back, both_sem.at[2], both_sem.at[3], other_core)
-    for n in range(1, nz):
-
-        @pl.when((core == 1) & (z < n))
-        def _():
-            wait_bytes(z_back.at[n], stat_tail_recv.at[n])
-
     @pl.when(core == 1)
     def _():
-        back_share.start()
         all_share.wait_recv()
         back_share.wait_send()
 
     @pl.when(core == 0)
     def _():
-        wait_bytes(z_all.at[0 : nz - 1], stat_recv.at[1])
-        all_share.start()
         back_share.wait_recv()
         all_share.wait_send()
 

time: 41.4 us -> 41.4 us (level)
  no operation moved by 1% of the time
where the time goes in v5:
time: 41.4 us; the launch traced here: 41.1 us
  Pallas kernels  39.8 us (96%)
  between operations  1.29 us (3%)
    pallas_call x1, Pallas kernels, local(): pl.pallas_call(functools.partial(kernel, (nz, nx, ny)), name='step', out_...  38.7 us
    pallas_call x1, Pallas kernels, local(): pl.pallas_call(finish, name='finish', out_shape=(fields_shape, node_shape...  1.15 us

profile of v5, /device:TPU:1, one launch (start us, length us, event | category | flops | bytes accessed | tf_op | source)
XLA Modules:
  0.0 41.1 jit_solution(18179999666071838783)
XLA Ops:
  1.3 38.7 %step.1 = (f32[2560,128]{1,0:T(8,128)S(1)}, f32[512,128]{1,0:T(8,128)S(1)}, f32[8,128]{1,0:T(8,128)S(1)}) custom-call(f32[2560,128]{1,0:T(8,128)} %bitcast.9, f32[512,128]{1,0:T(8,128)} %bitcast.10, f32[3,1,128]{2,1,0:T(1,128)} %metric.1, f32[5]{0:T(128)} %diffusivity.1, s32[1]{0:T(128)S(6)} %copy.10.flip, f32[8,128]{1,0:T(8,128)} %bitcast.11), custom_call_target="tpu_custom_call" | custom-call | tf_op jit(solution)/shard_map/step/pallas_call | solution.py:800
  40.0 1.2 %finish.1 = (f32[2560,128]{1,0:T(8,128)}, f32[512,128]{1,0:T(8,128)}) custom-call(f32[2560,128]{1,0:T(8,128)S(1)} %get-tuple-element.7.adv, f32[512,128]{1,0:T(8,128)S(1)} %get-tuple-element.8.guess, f32[8,128]{1,0:T(8,128)S(1)} %get-tuple-element.9.back), custom_call_target="tpu_custom_call" | custom-call | tf_op jit(solution)/shard_map/finish/pallas_call | solution.py:848
